TPU v7x, 32 devices: a whole 2x2x4 slice. The times are simulated.
32 devices in a mesh: dp: 8 (over z, y), blk: 4 (over x, core).
Axes of the slice: x: 2, y: 2, z: 4, core: 2. Of those that a mesh axis runs over, the one named last changes fastest.
Arguments:
- grads: bfloat16 [8, 4, 1024, 1024], P('dp', None, None, 'blk'), may hold values from -4 to 4
- left_old: float32 [4, 1024, 1024], P('blk', 'dp'), may hold values from -0.3 to 0.3
- right_old: float32 [4, 1024, 1024], P('blk', 'dp'), may hold values from -0.3 to 0.3
- left_root: bfloat16 [4, 1024, 1024], P('blk'), may hold values from -0.1875 to 0.1875
- right_root: bfloat16 [4, 1024, 1024], P('blk'), may hold values from -0.1875 to 0.1875
Outputs:
- update: bfloat16 [4, 1024, 1024], P(None, 'dp', 'blk')
- left_stat: float32 [4, 1024, 1024], P('blk', 'dp')
- right_stat: float32 [4, 1024, 1024], P('blk', 'dp')
All inputs are finite; a program needn't handle non-finite values.
Results may differ from a plain program's by a relative error of at most 0.0059.
Values may be sent and summed in bfloat16 or wider, within the bound.
No kernel may reach another device: no remote copies, remote signals or barrier semaphores. Data moves between devices by JAX's collectives and lax.ppermute only.
A program may use at most 64 MiB of HBM per device.

v0:
```python
import jax
import jax.numpy as jnp
from jax import lax
from jax.sharding import PartitionSpec as P

stat_decay = 0.9


def on_device(grads, left_old, right_old, left_root, right_root):
    block_size = left_root.shape[-1]
    strip_rows = left_old.shape[1]
    dp_index = lax.axis_index("dp")
    member_terms = grads[0].astype(jnp.float32)
    fsdp_shard = lax.psum_scatter(member_terms, "dp", scatter_dimension=1, tiled=True).astype(
        jnp.bfloat16
    )
    owned_rows = lax.all_to_all(fsdp_shard, "blk", split_axis=0, concat_axis=2, tiled=True)
    root_rows = lax.dynamic_slice_in_dim(left_root, dp_index * strip_rows, strip_rows, 1)
    whole_block = lax.all_gather(owned_rows, "dp", axis=1, tiled=True)
    own_columns = lax.dynamic_slice_in_dim(whole_block, dp_index * strip_rows, strip_rows, 2)
    left_prod = jnp.einsum(
        "bik,bjk->bij", owned_rows, whole_block, preferred_element_type=jnp.float32
    )
    right_prod = jnp.einsum(
        "bki,bkj->bij", own_columns, whole_block, preferred_element_type=jnp.float32
    )
    mid_prod = jnp.einsum(
        "bik,bkj->bij", root_rows, whole_block, preferred_element_type=jnp.float32
    )
    stat_scale = (1.0 - stat_decay) / block_size
    left_stat = stat_decay * left_old + stat_scale * left_prod
    right_stat = stat_decay * right_old + stat_scale * right_prod
    half_done = mid_prod.astype(jnp.bfloat16)
    owner_update = jnp.einsum(
        "bik,bkj->bij", half_done, right_root, preferred_element_type=jnp.float32
    ).astype(jnp.bfloat16)
    fsdp_update = lax.all_to_all(owner_update, "blk", split_axis=2, concat_axis=0, tiled=True)
    return (fsdp_update, left_stat, right_stat)


def solution(mesh):
    placed = (
        P("dp", None, None, "blk"),
        P("blk", "dp", None),
        P("blk", "dp", None),
        P("blk", None, None),
        P("blk", None, None),
    )
    return jax.shard_map(
        on_device,
        mesh=mesh,
        in_specs=placed,
        out_specs=(P(None, "dp", "blk"), P("blk", "dp", None), P("blk", "dp", None)),
        check_vma=False,
    )
```

profile of v0, /device:TPU:0, one launch (start us, length us, event | category | flops | bytes accessed | tf_op | source)
XLA Modules:
  0.0 191.3 jit_solution(13728316676888720214)
XLA Ops:
  7.2 0.0 copy-start
  7.2 0.0 reduce-scatter.2.cloned.1.call-start
  7.2 4.2 %copy.14 = bf16[1,4,1024,256]{2,3,1,0:T(8,128)(2,1)} copy(bf16[1,4,1024,256]{3,2,1,0:T(8,128)(2,1)} %param.5) | data formatting | bytes 4194304 | tf_op args[0]
  11.4 4.0 %bitcast_convert_fusion = f32[4,1024,256]{1,2,0:T(8,128)} fusion(bf16[1,4,1024,256]{2,3,1,0:T(8,128)(2,1)} %copy.14), kind=kLoop, calls=%fused_computation | loop fusion | flops 1048576 | bytes 6291456 | tf_op jit(solution)/shard_map/convert_element_type | solution.py:13
  15.4 0.0 reduce-scatter.2.cloned.1.call-update
  15.4 0.0 all-gather.2.cloned.1.call-start
  15.5 91.3 %reduce-scatter.2.cloned.1.call-done = f32[4,128,256]{1,2,0:T(8,128)} async-done(((f32[4,1024,256]{1,2,0:T(8,128)}), f32[4,128,256]{1,2,0:T(8,128)}) %reduce-scatter.2.cloned.1.call-update) | async-done | bytes 524304 | tf_op jit(solution)/shard_map/reduce_scatter | solution.py:14
  106.8 1.1 convert_element_type.21
  107.8 9.1 %all_to_all.36 = bf16[4,128,256]{1,2,0:T(8,128)(2,1)} all-to-all(bf16[4,128,256]{1,2,0:T(8,128)(2,1)S(1)} %convert_element_type.21), channel_id=1, replica_groups=mesh['dp'=8,'blk'=4] {'blk'}, dimensions={0} | all-to-all | bytes 524288 | tf_op jit(solution)/shard_map/all_to_all | solution.py:17
  116.9 0.0 all-gather.2.cloned.1.call-update
  117.0 50.1 %all-gather.2.cloned.1.call-done = bf16[1,1024,1024]{1,2,0:T(8,128)(2,1)} async-done(((bf16[1,128,1024]{1,2,0:T(8,128)(2,1)}), bf16[1,1024,1024]{1,2,0:T(8,128)(2,1)}) %all-gather.2.cloned.1.call-update) | async-done | bytes 2097168 | tf_op jit(solution)/shard_map/all_gather | solution.py:19
  167.0 0.0 copy-done
  167.0 2.8 %fusion.32 = bf16[1,128,1024]{2,1,0:T(8,128)(2,1)S(1)} fusion(bf16[1,1024,1024]{2,1,0:T(8,128)(2,1)S(1)} %copy-done, bf16[1,1024,1024]{1,2,0:T(8,128)(2,1)} %all-gather.2.cloned.1.call-done, bf16[1,1024,1024]{2,1,0:T(8,128)(2,1)} %param.8, s32[]{:T(128)S(6)} %select_n.4), kind=kOutput, calls=%fused_computation.17 | convolution fusion | flops 537133056 | bytes 4718596 | tf_op jit(solution)/shard_map/bik,bkj->bij/dot_general | solution.py:34
  169.9 0.0 copy-start.2
  169.9 0.4 copy.15
  170.3 0.5 broadcast.14
  170.8 2.2 %reduce = bf16[1024,128]{1,0:T(8,128)(2,1)S(1)} reduce(bf16[1024,1,128]{2,1,0:T(2,128)(2,1)S(1)} %bitcast.68, bf16[]{:T(256)} %broadcast.14), dimensions={1}, to_apply=%bitcast.62.reduce_sub_computation | reduce | bytes 524290
  173.0 0.8 reshape.42
  173.8 0.0 copy-start.3
  173.8 3.5 %all-to-all-start.1 = ((bf16[4,2,16384]{2,1,0:T(2,128)(2,1)}), bf16[4,2,16384]{2,1,0:T(2,128)(2,1)S(1)}, u32[]{:S(2)}, u32[]{:S(2)}) async-start(bf16[4,2,16384]{2,1,0:T(2,128)(2,1)} %reshape.42), calls=%async_computation.2 | async-start | bytes 524288 | tf_op jit(solution)/shard_map/all_to_all | solution.py:37
  177.3 0.0 copy-start.1
  177.3 0.0 copy-done.2
  177.3 3.1 %fusion.23 = f32[1,128,1024]{2,1,0:T(8,128)} fusion(bf16[128,1024]{0,1:T(8,128)(2,1)S(1)} %bitcast.66, bf16[1,1024,1024]{1,2,0:T(8,128)(2,1)} %all-gather.2.cloned.1.call-done, f32[1,128,1024]{2,1,0:T(8,128)} %param.6), kind=kOutput, calls=%fused_computation.14 | convolution fusion | flops 268828672 | bytes 3407872 | tf_op jit(solution)/shard_map/bik,bjk->bij/dot_general | solution.py:21
  180.4 0.0 copy-done.3
  180.4 0.0 copy-done.1
  180.4 1.6 fusion.20
  182.1 1.2 all-to-all-done.1
  183.3 0.3 reshape.43
  183.6 0.9 copy.16
  (1 shorter events, 0.0 us)
Async XLA Ops:
  7.2 159.9 %copy-start = (bf16[1,1024,1024]{2,1,0:T(8,128)(2,1)S(1)}, bf16[1,1024,1024]{2,1,0:T(8,128)(2,1)}, u32[]{:S(2)}) copy-start(bf16[1,1024,1024]{2,1,0:T(8,128)(2,1)} %param.9) | copy-start | bytes 6291460
  7.2 99.6 %reduce-scatter.2.cloned.1.call-start = ((), (), s32[]{:S(2)}) async-start(), calls=%async_computation.3 | async-start | bytes 4718592 | tf_op jit(solution)/shard_map/reduce_scatter | solution.py:14
  15.4 151.6 %all-gather.2.cloned.1.call-start = ((), (), s32[]{:S(2)}) async-start(), calls=%async_computation.4 | async-start | bytes 2359296 | tf_op jit(solution)/shard_map/all_gather | solution.py:19
  169.9 7.5 %copy-start.2 = (bf16[4,128,256]{1,2,0:T(8,128)(2,1)S(1)}, bf16[4,128,256]{1,2,0:T(8,128)(2,1)}, u32[]{:S(2)}) copy-start(bf16[4,128,256]{1,2,0:T(8,128)(2,1)} %all_to_all.36) | copy-start | bytes 786436
  173.8 6.7 %copy-start.3 = (f32[1,128,1024]{2,1,0:T(8,128)S(1)}, f32[1,128,1024]{2,1,0:T(8,128)}, u32[]{:S(2)}) copy-start(f32[1,128,1024]{2,1,0:T(8,128)} %param.7) | copy-start | bytes 1572868
  173.8 9.5 %all-to-all-start.1 = ((bf16[4,2,16384]{2,1,0:T(2,128)(2,1)}), bf16[4,2,16384]{2,1,0:T(2,128)(2,1)S(1)}, u32[]{:S(2)}, u32[]{:S(2)}) async-start(bf16[4,2,16384]{2,1,0:T(2,128)(2,1)} %reshape.42), calls=%async_computation.2 | async-start | bytes 524288 | tf_op jit(solution)/shard_map/all_to_all | solution.py:37
  177.3 3.1 %copy-start.1 = (bf16[1,1024,1024]{1,2,0:T(8,128)(2,1)S(1)}, bf16[1,1024,1024]{1,2,0:T(8,128)(2,1)}, u32[]{:S(2)}) copy-start(bf16[1,1024,1024]{1,2,0:T(8,128)(2,1)} %all-gather.2.cloned.1.call-done) | copy-start | bytes 6291460
Sparse Core Ops, SparseCore 0:
  15.5 91.1 reduce-scatter.1
  117.1 49.9 all-gather.1
where the time goes:
time: 192 us; the launch traced here: 191 us
  waiting for transfers between devices  143 us (74%)
  between operations  14.1 us (7%)
  blocking collectives  9.1 us (5%)
  matrix products  7.55 us (4%)
  other arithmetic  7.29 us (4%)
  local copies, waits for them, and re-layouts  7.02 us (4%)
  starting transfers between devices  3.62 us (2%)
    reduce_scatter x1, waiting for transfers between devices, on_device(): lax.psum_scatter(member_terms, 'dp', scatter_dimension=1, tiled=True)  91.3 us
    all_gather x1, waiting for transfers between devices, on_device(): whole_block = lax.all_gather(owned_rows, 'dp', axis=1, tiled=True)  50.1 us
    all_to_all x1, blocking collectives, on_device(): lax.all_to_all(fsdp_shard, 'blk', split_axis=0, concat_axis=2, tiled=True)  9.1 us
    unnamed x14, local copies, waits for them, and re-layouts  6.63 us
    convert_element_type x1, other arithmetic, on_device(): member_terms = grads[0].astype(jnp.float32)  4 us
  transfers between devices with their start and end apart: 3, of which 3 were waited for; matrix products, arithmetic and copies ran while one was open for 2% of the time, Pallas kernels for 0%

commit v1 on v0

v1 whole, which is shorter than its diff:
```python
import jax
import jax.numpy as jnp
from jax import lax
from jax.sharding import PartitionSpec as P

stat_decay = 0.9
chunk_parts = (3, 3, 2)


def swap(values, axis, mask):
    size = lax.axis_size(axis)
    return lax.ppermute(values, axis, [(i, i ^ mask) for i in range(size)])


def pick(values, index, dim):
    return lax.dynamic_index_in_dim(values, index, dim, keepdims=False)


def ordered(pieces, index):
    count = len(pieces)
    return [
        lax.select_n(index, *[pieces[place ^ me] for me in range(count)])
        for place in range(count)
    ]


def chunks_of(rows):
    total = sum(chunk_parts)
    edges = [0]
    for part in chunk_parts:
        edges.append(edges[-1] + rows * part // total)
    return list(zip(edges[:-1], edges[1:]))


def on_device(grads, left_old, right_old, left_root, right_root):
    members, owners = lax.axis_size("dp"), lax.axis_size("blk")
    near = members // 2
    block_size = left_root.shape[-1]
    strip_rows = left_old.shape[1]
    dp_index = lax.axis_index("dp")
    blk_index = lax.axis_index("blk")
    low = dp_index % near
    depth = block_size // near
    cols = grads.shape[3]
    split = grads[0].reshape(owners, near, depth, cols)

    spans = chunks_of(depth)
    firsts = []
    for start, stop in spans:
        part = split[:, :, start:stop]
        firsts.append(
            [swap(pick(part, low ^ m, 1), "dp", m) for m in range(1, near)]
        )
    gathered = []
    for (start, stop), first in zip(spans, firsts):
        part = split[:, :, start:stop]
        near_sum = pick(part, low, 1).astype(jnp.float32)
        for piece in first:
            near_sum = near_sum + piece.astype(jnp.float32)
        far = swap(near_sum.astype(jnp.bfloat16), "dp", near)
        owned = (near_sum + far.astype(jnp.float32)).astype(jnp.bfloat16)
        pieces = [pick(owned, blk_index, 0)] + [
            swap(pick(owned, blk_index ^ m, 0), "blk", m) for m in range(1, owners)
        ]
        strip = jnp.concatenate(ordered(pieces, blk_index), axis=1)[None]
        mask = near // 2
        while mask:
            other = swap(strip, "dp", mask)
            strip = jnp.concatenate(ordered([strip, other], (low // mask) % 2), axis=0)
            mask //= 2
        gathered.append(strip)
    places = [0]
    mask = near // 2
    while mask:
        places = places + [p + mask for p in places]
        mask //= 2
    whole = jnp.concatenate(gathered, axis=1)
    order = [places.index(p) for p in range(near)]
    whole = jnp.concatenate([whole[i] for i in order], axis=0)

    own_rows = lax.dynamic_slice_in_dim(whole, dp_index * strip_rows, strip_rows, 0)
    own_columns = lax.dynamic_slice_in_dim(whole, dp_index * strip_rows, strip_rows, 1)
    root_rows = lax.dynamic_slice_in_dim(left_root[0], dp_index * strip_rows, strip_rows, 0)
    half_done = jnp.dot(root_rows, whole, preferred_element_type=jnp.float32).astype(jnp.bfloat16)
    owner_update = jnp.dot(half_done, right_root[0], preferred_element_type=jnp.float32).astype(
        jnp.bfloat16
    )
    by_columns = owner_update.reshape(strip_rows, owners, cols)
    back = [pick(by_columns, blk_index, 1)] + [
        swap(pick(by_columns, blk_index ^ m, 1), "blk", m) for m in range(1, owners)
    ]
    update = jnp.stack(ordered(back, blk_index))
    left_prod = jnp.einsum("ik,jk->ij", own_rows, whole, preferred_element_type=jnp.float32)
    right_prod = jnp.einsum("ki,kj->ij", own_columns, whole, preferred_element_type=jnp.float32)
    stat_scale = (1.0 - stat_decay) / block_size
    left_stat = stat_decay * left_old + stat_scale * left_prod
    right_stat = stat_decay * right_old + stat_scale * right_prod
    return (update, left_stat, right_stat)


def solution(mesh):
    placed = (
        P("dp", None, None, "blk"),
        P("blk", "dp", None),
        P("blk", "dp", None),
        P("blk", None, None),
        P("blk", None, None),
    )
    return jax.shard_map(
        on_device,
        mesh=mesh,
        in_specs=placed,
        out_specs=(P(None, "dp", "blk"), P("blk", "dp", None), P("blk", "dp", None)),
        check_vma=False,
    )
```

time: 192 us -> 97.7 us (0.51)
  waiting for transfers between devices: 143 us -> 34.9 us
  starting transfers between devices: 3.62 us -> 36.9 us
  between operations: 14.1 us -> 1.03 us
  blocking collectives: 9.1 us -> 0 us
  other arithmetic: 7.29 us -> 10.6 us
    reduce_scatter x1 -> x0, waiting for transfers between devices: 91.3 us -> none  [on_device(): lax.psum_scatter(member_terms, 'dp', scatter_dimension=1, tiled=True)]
    all_gather x1 -> x0, waiting for transfers between devices: 50.1 us -> none  [on_device(): whole_block = lax.all_gather(owned_rows, 'dp', axis=1, tiled=True)]
    ppermute x0 -> x30, starting transfers between devices: none -> 36.9 us  [swap(): return lax.ppermute(values, axis, [(i, i ^ mask) for i in range(size)])]
    ppermute x0 -> x30, waiting for transfers between devices: none -> 34.9 us  [swap(): return lax.ppermute(values, axis, [(i, i ^ mask) for i in range(size)])]
    all_to_all x1 -> x0, blocking collectives: 9.1 us -> none  [on_device(): lax.all_to_all(fsdp_shard, 'blk', split_axis=0, concat_axis=2, tiled=True)]
    unnamed x14 -> x17, local copies, waits for them, and re-layouts: 6.63 us -> 1.9 us
    all_to_all x1 -> x0, starting transfers between devices: 3.54 us -> none  [on_device(): lax.all_to_all(owner_update, 'blk', split_axis=2, concat_axis=0, tiled=True)]
    slice x0 -> x2, local copies, waits for them, and re-layouts: none -> 2.73 us  [on_device(): part = split[:, :, start:stop]]
  transfers between devices with their start and end apart: 3 -> 30, of which waited for: 3 -> 10; matrix products, arithmetic and copies ran while one was open for 2% -> 15% of each run, Pallas kernels for 0% -> 0%
where the time goes in v1:
time: 97.7 us; the launch traced here: 97.3 us
  starting transfers between devices  36.9 us (38%)
  waiting for transfers between devices  34.9 us (36%)
  other arithmetic  10.6 us (11%)
  local copies, waits for them, and re-layouts  7.22 us (7%)
  matrix products  6.64 us (7%)
  between operations  1.03 us (1%)
    ppermute x30, starting transfers between devices, swap(): return lax.ppermute(values, axis, [(i, i ^ mask) for i in range(size)])  36.9 us
    ppermute x30, waiting for transfers between devices, swap(): return lax.ppermute(values, axis, [(i, i ^ mask) for i in range(size)])  34.9 us
    dot_general x1, matrix products, on_device(): jnp.einsum('ik,jk->ij', own_rows, whole, preferred_element_type=jnp.float32)  3.33 us
    slice x2, local copies, waits for them, and re-layouts, on_device(): part = split[:, :, start:stop]  2.73 us
    convert_element_type x3, other arithmetic, on_device(): owned = (near_sum + far.astype(jnp.float32)).astype(jnp.bfloat16)  2.44 us
    select_n x8, other arithmetic, ordered(): lax.select_n(index, *[pieces[place ^ me] for me in range(count)])  2.39 us
    convert_element_type x3, other arithmetic, on_device(): far = swap(near_sum.astype(jnp.bfloat16), 'dp', near)  2.37 us
    dot_general x1, matrix products, on_device(): jnp.dot(half_done, right_root[0], preferred_element_type=jnp.float32)  2.04 us
  transfers between devices with their start and end apart: 30, of which 10 were waited for; matrix products, arithmetic and copies ran while one was open for 15% of the time, Pallas kernels for 0%

profile of v1, /device:TPU:0, one launch (start us, length us, event | category | flops | bytes accessed | tf_op | source)
XLA Modules:
  0.0 97.3 jit_solution(12562384852249874867)
XLA Ops:
  0.7 1.2 %slice.33 = bf16[4,4,64,256]{3,2,1,0:T(8,128)(2,1)S(1)} slice(bf16[4,4,256,256]{3,2,1,0:T(8,128)(2,1)} %bitcast.162), slice={[0:4], [0:4], [192:256], [0:256]} | slice | bytes 1048576 | tf_op jit(solution)/shard_map/slice | solution.py:56
  2.7 4.0 %collective-permute-start.20 = (bf16[4,64,256]{2,1,0:T(8,128)(2,1)}, bf16[4,64,256]{2,1,0:T(8,128)(2,1)S(1)}, u32[]{:S(2)}, u32[]{:S(2)}) collective-permute-start(bf16[4,64,256]{2,1,0:T(8,128)(2,1)} %get-tuple-element.24), channel_id=1, source_target_pairs={{0,12},{4,8},{8,4},{12,0},{16,28},{20,24},{24,20},{28,16},{1,13},{... | collective-permute-start | bytes 393224 | tf_op jit(solution)/shard_map/ppermute | solution.py:12
  7.2 1.5 %fusion.40 = (bf16[4,4,96,256]{3,2,1,0:T(8,128)(2,1)S(1)}, bf16[4,4,96,256]{3,2,1,0:T(8,128)(2,1)S(1)}) fusion(bf16[4,4,256,256]{3,2,1,0:T(8,128)(2,1)} %bitcast.163), kind=kLoop, calls=%fused_computation.111 | loop fusion | bytes 3145728 | tf_op jit(solution)/shard_map/slice | solution.py:56
  10.5 2.9 %collective-permute-start.11 = (bf16[4,96,256]{2,1,0:T(8,128)(2,1)}, bf16[4,96,256]{2,1,0:T(8,128)(2,1)}, u32[]{:S(2)}, u32[]{:S(2)}) collective-permute-start(bf16[4,96,256]{2,1,0:T(8,128)(2,1)} %get-tuple-element.19), channel_id=1, source_target_pairs={{0,12},{4,8},{8,4},{12,0},{16,28},{20,24},{24,20},{28,16},{1,13},{... | collective-permute-start | bytes 589832 | tf_op jit(solution)/shard_map/ppermute | solution.py:12
  14.1 2.9 %collective-permute-start.2 = (bf16[4,96,256]{2,1,0:T(8,128)(2,1)S(1)}, bf16[4,96,256]{2,1,0:T(8,128)(2,1)S(1)}, u32[]{:S(2)}, u32[]{:S(2)}) collective-permute-start(bf16[4,96,256]{2,1,0:T(8,128)(2,1)S(1)} %get-tuple-element.14), channel_id=1, source_target_pairs={{0,12},{4,8},{8,4},{12,0},{16,28},{20,24},{24,20},{28,16},{1,13},{... | collective-permute-start | bytes 589832 | tf_op jit(solution)/shard_map/ppermute | solution.py:12
  19.5 1.9 %collective-permute-start = (bf16[4,96,256]{2,1,0:T(8,128)(2,1)S(1)}, bf16[4,96,256]{2,1,0:T(8,128)(2,1)S(1)}, u32[]{:S(2)}, u32[]{:S(2)}) collective-permute-start(bf16[4,96,256]{2,1,0:T(8,128)(2,1)S(1)} %get-tuple-element.13), channel_id=1, source_target_pairs={{0,4},{4,0},{8,12},{12,8},{16,20},{20,16},{24,28},{28,24},{1,5},{5... | collective-permute-start | bytes 589832 | tf_op jit(solution)/shard_map/ppermute | solution.py:12
  21.4 4.2 %collective-permute-done.10 = bf16[4,96,256]{2,1,0:T(8,128)(2,1)} collective-permute-done((bf16[4,96,256]{2,1,0:T(8,128)(2,1)}, bf16[4,96,256]{2,1,0:T(8,128)(2,1)}, u32[]{:S(2)}, u32[]{:S(2)}) %collective-permute-start.10) | collective-permute-done | bytes 196640 | tf_op jit(solution)/shard_map/ppermute | solution.py:12
  25.6 1.2 %collective-permute-start.21 = (bf16[4,64,256]{2,1,0:T(8,128)(2,1)S(1)}, bf16[4,64,256]{2,1,0:T(8,128)(2,1)S(1)}, u32[]{:S(2)}, u32[]{:S(2)}) collective-permute-start(bf16[4,64,256]{2,1,0:T(8,128)(2,1)S(1)} %fusion.23), channel_id=1, source_target_pairs={{0,16},{4,20},{8,24},{12,28},{16,0},{20,4},{24,8},{28,12},{1,17},{... | collective-permute-start | bytes 393224 | tf_op jit(solution)/shard_map/ppermute | solution.py:12
  26.8 1.2 %fusion.22 = bf16[4,96,256]{2,1,0:T(8,128)(2,1)S(1)} fusion(bf16[4,96,256]{2,1,0:T(8,128)(2,1)} %collective-permute-done.11, bf16[4,96,256]{2,1,0:T(8,128)(2,1)} %collective-permute-done.10, bf16[4,96,256]{2,1,0:T(8,128)(2,1)S(1)} %collective-permute-done.9, bf16[4,4,96,256]{3,2,1,0:T(8,128)(2,1)} %copy-done.2, s32[]{:T(128)S(6)} %select_n.437), kind=kLoop, calls=%fused_computation.61 | loop fusion | flops 786432 | bytes 983044 | tf_op jit(solution)/shard_map/convert_element_type | solution.py:60
  28.0 2.1 %collective-permute-start.12 = (bf16[4,96,256]{2,1,0:T(8,128)(2,1)S(1)}, bf16[4,96,256]{2,1,0:T(8,128)(2,1)S(1)}, u32[]{:S(2)}, u32[]{:S(2)}) collective-permute-start(bf16[4,96,256]{2,1,0:T(8,128)(2,1)S(1)} %fusion.22), channel_id=1, source_target_pairs={{0,16},{4,20},{8,24},{12,28},{16,0},{20,4},{24,8},{28,12},{1,17},{... | collective-permute-start | bytes 589832 | tf_op jit(solution)/shard_map/ppermute | solution.py:12
  30.2 4.3 %collective-permute-done.21 = bf16[4,64,256]{2,1,0:T(8,128)(2,1)S(1)} collective-permute-done((bf16[4,64,256]{2,1,0:T(8,128)(2,1)S(1)}, bf16[4,64,256]{2,1,0:T(8,128)(2,1)S(1)}, u32[]{:S(2)}, u32[]{:S(2)}) %collective-permute-start.21) | collective-permute-done | bytes 131104 | tf_op jit(solution)/shard_map/ppermute | solution.py:12
  34.5 1.1 %add_convert_fusion.2 = bf16[4,64,256]{2,1,0:T(8,128)(2,1)S(1)} fusion(bf16[4,64,256]{2,1,0:T(8,128)(2,1)S(1)} %collective-permute-done.21, bf16[4,64,256]{2,1,0:T(8,128)(2,1)S(1)} %collective-permute-done.20, bf16[4,64,256]{2,1,0:T(8,128)(2,1)} %collective-permute-done.19, bf16[4,64,256]{2,1,0:T(8,128)(2,1)} %collective-permute-done.18, ...), kind=kLoop, calls=%fused_computation.38 | loop fusion | flops 655360 | bytes 786436 | tf_op jit(solution)/shard_map/convert_element_type | solution.py:61
  35.6 1.6 %collective-permute-start.23 = (bf16[64,256]{1,0:T(8,128)(2,1)S(1)}, bf16[64,256]{1,0:T(8,128)(2,1)S(1)}, u32[]{:S(2)}, u32[]{:S(2)}) collective-permute-start(bf16[64,256]{1,0:T(8,128)(2,1)S(1)} %get-tuple-element.57), channel_id=1, source_target_pairs={{0,2},{1,3},{2,0},{3,1},{4,6},{5,7},{6,4},{7,5},{8,10},{9,11},{10,... | collective-permute-start | bytes 98312 | tf_op jit(solution)/shard_map/ppermute | solution.py:12
  37.6 3.5 %collective-permute-start.3 = (bf16[4,96,256]{2,1,0:T(8,128)(2,1)S(1)}, bf16[4,96,256]{2,1,0:T(8,128)(2,1)S(1)}, u32[]{:S(2)}, u32[]{:S(2)}) collective-permute-start(bf16[4,96,256]{2,1,0:T(8,128)(2,1)S(1)} %fusion.21), channel_id=1, source_target_pairs={{0,16},{4,20},{8,24},{12,28},{16,0},{20,4},{24,8},{28,12},{1,17},{... | collective-permute-start | bytes 589832 | tf_op jit(solution)/shard_map/ppermute | solution.py:12
  41.2 3.9 %collective-permute-start.25 = (bf16[1,64,1024]{2,1,0:T(8,128)(2,1)S(1)}, bf16[1,64,1024]{2,1,0:T(8,128)(2,1)S(1)}, u32[]{:S(2)}, u32[]{:S(2)}) collective-permute-start(bf16[1,64,1024]{2,1,0:T(8,128)(2,1)S(1)} %maximum_bitcast_fusion.2), channel_id=1, source_target_pairs={{0,8},{4,12},{8,0},{12,4},{16,24},{20,28},{24,16},{28,20},{1,9},{5... | collective-permute-start | bytes 393224 | tf_op jit(solution)/shard_map/ppermute | solution.py:12
  45.1 1.2 %add_convert_fusion = bf16[4,96,256]{2,1,0:T(8,128)(2,1)S(1)} fusion(bf16[4,96,256]{2,1,0:T(8,128)(2,1)S(1)} %collective-permute-done.12, bf16[4,96,256]{2,1,0:T(8,128)(2,1)} %collective-permute-done.11, bf16[4,96,256]{2,1,0:T(8,128)(2,1)} %collective-permute-done.10, bf16[4,96,256]{2,1,0:T(8,128)(2,1)S(1)} %collective-permute-done.9, ...), kind=kLoop, calls=%fused_computation.24 | loop fusion | flops 983040 | bytes 1179652 | tf_op jit(solution)/shard_map/convert_element_type | solution.py:61
  46.4 1.6 %collective-permute-start.14 = (bf16[96,256]{1,0:T(8,128)(2,1)S(1)}, bf16[96,256]{1,0:T(8,128)(2,1)S(1)}, u32[]{:S(2)}, u32[]{:S(2)}) collective-permute-start(bf16[96,256]{1,0:T(8,128)(2,1)S(1)} %get-tuple-element.54), channel_id=1, source_target_pairs={{0,2},{1,3},{2,0},{3,1},{4,6},{5,7},{6,4},{7,5},{8,10},{9,11},{10,... | collective-permute-start | bytes 147464 | tf_op jit(solution)/shard_map/ppermute | solution.py:12
  48.3 2.4 %collective-permute-done.3 = bf16[4,96,256]{2,1,0:T(8,128)(2,1)S(1)} collective-permute-done((bf16[4,96,256]{2,1,0:T(8,128)(2,1)S(1)}, bf16[4,96,256]{2,1,0:T(8,128)(2,1)S(1)}, u32[]{:S(2)}, u32[]{:S(2)}) %collective-permute-start.3) | collective-permute-done | bytes 196640 | tf_op jit(solution)/shard_map/ppermute | solution.py:12
  51.0 1.6 %collective-permute-start.5 = (bf16[96,256]{1,0:T(8,128)(2,1)S(1)}, bf16[96,256]{1,0:T(8,128)(2,1)S(1)}, u32[]{:S(2)}, u32[]{:S(2)}) collective-permute-start(bf16[96,256]{1,0:T(8,128)(2,1)S(1)} %get-tuple-element.51), channel_id=1, source_target_pairs={{0,2},{1,3},{2,0},{3,1},{4,6},{5,7},{6,4},{7,5},{8,10},{9,11},{10,... | collective-permute-start | bytes 147464 | tf_op jit(solution)/shard_map/ppermute | solution.py:12
  53.8 1.4 %collective-permute-done.5 = bf16[96,256]{1,0:T(8,128)(2,1)S(1)} collective-permute-done((bf16[96,256]{1,0:T(8,128)(2,1)S(1)}, bf16[96,256]{1,0:T(8,128)(2,1)S(1)}, u32[]{:S(2)}, u32[]{:S(2)}) %collective-permute-start.5) | collective-permute-done | bytes 49184 | tf_op jit(solution)/shard_map/ppermute | solution.py:12
  55.1 1.1 %collective-permute-done.6 = bf16[96,256]{1,0:T(8,128)(2,1)S(1)} collective-permute-done((bf16[96,256]{1,0:T(8,128)(2,1)S(1)}, bf16[96,256]{1,0:T(8,128)(2,1)S(1)}, u32[]{:S(2)}, u32[]{:S(2)}) %collective-permute-start.6) | collective-permute-done | bytes 49184 | tf_op jit(solution)/shard_map/ppermute | solution.py:12
  58.0 1.1 %collective-permute-start.26 = (bf16[2,64,1024]{2,1,0:T(8,128)(2,1)}, bf16[2,64,1024]{2,1,0:T(8,128)(2,1)}, u32[]{:S(2)}, u32[]{:S(2)}) collective-permute-start(bf16[2,64,1024]{2,1,0:T(8,128)(2,1)} %pad_maximum_fusion.3), channel_id=1, source_target_pairs={{0,4},{4,0},{8,12},{12,8},{16,20},{20,16},{24,28},{28,24},{1,5},{5... | collective-permute-start | bytes 786440 | tf_op jit(solution)/shard_map/ppermute | solution.py:12
  59.0 1.7 %collective-permute-done.16 = bf16[1,96,1024]{2,1,0:T(8,128)(2,1)S(1)} collective-permute-done((bf16[1,96,1024]{2,1,0:T(8,128)(2,1)S(1)}, bf16[1,96,1024]{2,1,0:T(8,128)(2,1)S(1)}, u32[]{:S(2)}, u32[]{:S(2)}) %collective-permute-start.16) | collective-permute-done | bytes 196640 | tf_op jit(solution)/shard_map/ppermute | solution.py:12
  60.7 3.7 %collective-permute-done.7 = bf16[1,96,1024]{2,1,0:T(8,128)(2,1)S(1)} collective-permute-done((bf16[1,96,1024]{2,1,0:T(8,128)(2,1)S(1)}, bf16[1,96,1024]{2,1,0:T(8,128)(2,1)S(1)}, u32[]{:S(2)}, u32[]{:S(2)}) %collective-permute-start.7) | collective-permute-done | bytes 196640 | tf_op jit(solution)/shard_map/ppermute | solution.py:12
  64.6 1.4 %collective-permute-start.17 = (bf16[2,96,1024]{2,1,0:T(8,128)(2,1)S(1)}, bf16[2,96,1024]{2,1,0:T(8,128)(2,1)}, u32[]{:S(2)}, u32[]{:S(2)}) collective-permute-start(bf16[2,96,1024]{2,1,0:T(8,128)(2,1)S(1)} %pad_maximum_fusion.2), channel_id=1, source_target_pairs={{0,4},{4,0},{8,12},{12,8},{16,20},{20,16},{24,28},{28,24},{1,5},{5... | collective-permute-start | bytes 1179656 | tf_op jit(solution)/shard_map/ppermute | solution.py:12
  67.8 9.0 %collective-permute-done.17 = bf16[2,96,1024]{2,1,0:T(8,128)(2,1)} collective-permute-done((bf16[2,96,1024]{2,1,0:T(8,128)(2,1)S(1)}, bf16[2,96,1024]{2,1,0:T(8,128)(2,1)}, u32[]{:S(2)}, u32[]{:S(2)}) %collective-permute-start.17) | collective-permute-done | bytes 393248 | tf_op jit(solution)/shard_map/ppermute | solution.py:12
  77.8 6.1 %collective-permute-done.8 = bf16[2,96,1024]{2,1,0:T(8,128)(2,1)S(1)} collective-permute-done((bf16[2,96,1024]{2,1,0:T(8,128)(2,1)S(1)}, bf16[2,96,1024]{2,1,0:T(8,128)(2,1)S(1)}, u32[]{:S(2)}, u32[]{:S(2)}) %collective-permute-start.8) | collective-permute-done | bytes 393248 | tf_op jit(solution)/shard_map/ppermute | solution.py:12
  85.4 1.5 %pad_maximum_fusion = bf16[1024,1024]{1,0:T(8,128)(2,1)} fusion(bf16[256,1024]{1,0:T(8,128)(2,1)S(1)} %get-tuple-element.6, bf16[256,1024]{1,0:T(8,128)(2,1)S(1)} %get-tuple-element.7, bf16[256,1024]{1,0:T(8,128)(2,1)S(1)} %get-tuple-element.8, bf16[256,1024]{1,0:T(8,128)(2,1)S(1)} %get-tuple-element.5), kind=kLoop, calls=%fused_computation.1 | loop fusion | flops 8388608 | bytes 4194304 | tf_op jit(solution)/shard_map/concatenate | solution.py:79
  86.9 2.0 %fusion.6 = bf16[128,1024]{1,0:T(8,128)(2,1)S(1)} fusion(bf16[1,1024,1024]{2,1,0:T(8,128)(2,1)S(1)} %copy-done, bf16[1,1024,1024]{2,1,0:T(8,128)(2,1)} %param.8, s32[]{:T(128)S(6)} %select_n.426, bf16[256,1024]{1,0:T(8,128)(2,1)S(1)} %get-tuple-element.6, bf16[256,1024]{1,0:T(8,128)(2,1)} %copy-done.3, bf16[256,1024]{1,0:T(8,128)(2,1)} %copy-done.4, ...), kind=kOutput, calls=%fused_computation.10 | convolution fusion | flops 545521664 | bytes 4718596 | tf_op jit(solution)/shard_map/dot_general | solution.py:85
  89.8 1.4 %collective-permute-start.28 = (bf16[128,256]{1,0:T(8,128)(2,1)S(1)}, bf16[128,256]{1,0:T(8,128)(2,1)S(1)}, u32[]{:S(2)}, u32[]{:S(2)}) collective-permute-start(bf16[128,256]{1,0:T(8,128)(2,1)S(1)} %bitcast.165), channel_id=1, source_target_pairs={{0,2},{1,3},{2,0},{3,1},{4,6},{5,7},{6,4},{7,5},{8,10},{9,11},{10,... | collective-permute-start | bytes 196616 | tf_op jit(solution)/shard_map/ppermute | solution.py:12
  91.8 3.3 %fusion.4 = f32[1,128,1024]{2,1,0:T(8,128)} fusion(bf16[1024,1024]{1,0:T(8,128)(2,1)} %pad_maximum_fusion, f32[1,128,1024]{2,1,0:T(8,128)S(1)} %copy-done.5, s32[]{:T(128)S(6)} %select_n.426), kind=kOutput, calls=%fused_computation.8 | convolution fusion | flops 268828672 | bytes 3407876 | tf_op jit(solution)/shard_map/ik,jk->ij/dot_general | solution.py:93
  95.2 1.3 %fusion.5 = f32[1,128,1024]{2,1,0:T(8,128)} fusion(bf16[1024,1024]{1,0:T(8,128)(2,1)S(1)} %copy-done.1, f32[1,128,1024]{2,1,0:T(8,128)S(1)} %copy-done.6, s32[]{:T(128)S(6)} %select_n.426), kind=kOutput, calls=%fused_computation.9 | convolution fusion | flops 268828672 | bytes 3407876 | tf_op jit(solution)/shard_map/ki,kj->ij/dot_general | solution.py:94
  (84 shorter events, 17.0 us)
Async XLA Ops:
  0.6 86.3 %copy-start = (bf16[1,1024,1024]{2,1,0:T(8,128)(2,1)S(1)}, bf16[1,1024,1024]{2,1,0:T(8,128)(2,1)}, u32[]{:S(2)}) copy-start(bf16[1,1024,1024]{2,1,0:T(8,128)(2,1)} %param.9) | copy-start | bytes 6291460
  2.7 11.2 %collective-permute-start.20 = (bf16[4,64,256]{2,1,0:T(8,128)(2,1)}, bf16[4,64,256]{2,1,0:T(8,128)(2,1)S(1)}, u32[]{:S(2)}, u32[]{:S(2)}) collective-permute-start(bf16[4,64,256]{2,1,0:T(8,128)(2,1)} %get-tuple-element.24), channel_id=1, source_target_pairs={{0,12},{4,8},{8,4},{12,0},{16,28},{20,24},{24,20},{28,16},{1,13},{... | collective-permute-start | bytes 393224 | tf_op jit(solution)/shard_map/ppermute | solution.py:12
  6.7 7.4 %collective-permute-start.19 = (bf16[4,64,256]{2,1,0:T(8,128)(2,1)}, bf16[4,64,256]{2,1,0:T(8,128)(2,1)}, u32[]{:S(2)}, u32[]{:S(2)}) collective-permute-start(bf16[4,64,256]{2,1,0:T(8,128)(2,1)} %get-tuple-element.25), channel_id=1, source_target_pairs={{0,8},{4,12},{8,0},{12,4},{16,24},{20,28},{24,16},{28,20},{1,9},{5... | collective-permute-start | bytes 393224 | tf_op jit(solution)/shard_map/ppermute | solution.py:12
  7.1 9.9 %collective-permute-start.18 = (bf16[4,64,256]{2,1,0:T(8,128)(2,1)}, bf16[4,64,256]{2,1,0:T(8,128)(2,1)}, u32[]{:S(2)}, u32[]{:S(2)}) collective-permute-start(bf16[4,64,256]{2,1,0:T(8,128)(2,1)} %get-tuple-element.23), channel_id=1, source_target_pairs={{0,4},{4,0},{8,12},{12,8},{16,20},{20,16},{24,28},{28,24},{1,5},{5... | collective-permute-start | bytes 393224 | tf_op jit(solution)/shard_map/ppermute | solution.py:12
  10.5 9.1 %collective-permute-start.11 = (bf16[4,96,256]{2,1,0:T(8,128)(2,1)}, bf16[4,96,256]{2,1,0:T(8,128)(2,1)}, u32[]{:S(2)}, u32[]{:S(2)}) collective-permute-start(bf16[4,96,256]{2,1,0:T(8,128)(2,1)} %get-tuple-element.19), channel_id=1, source_target_pairs={{0,12},{4,8},{8,4},{12,0},{16,28},{20,24},{24,20},{28,16},{1,13},{... | collective-permute-start | bytes 589832 | tf_op jit(solution)/shard_map/ppermute | solution.py:12
  13.4 12.2 %collective-permute-start.10 = (bf16[4,96,256]{2,1,0:T(8,128)(2,1)}, bf16[4,96,256]{2,1,0:T(8,128)(2,1)}, u32[]{:S(2)}, u32[]{:S(2)}) collective-permute-start(bf16[4,96,256]{2,1,0:T(8,128)(2,1)} %get-tuple-element.20), channel_id=1, source_target_pairs={{0,8},{4,12},{8,0},{12,4},{16,24},{20,28},{24,16},{28,20},{1,9},{5... | collective-permute-start | bytes 589832 | tf_op jit(solution)/shard_map/ppermute | solution.py:12
  13.9 12.9 %collective-permute-start.9 = (bf16[4,96,256]{2,1,0:T(8,128)(2,1)}, bf16[4,96,256]{2,1,0:T(8,128)(2,1)S(1)}, u32[]{:S(2)}, u32[]{:S(2)}) collective-permute-start(bf16[4,96,256]{2,1,0:T(8,128)(2,1)} %get-tuple-element.18), channel_id=1, source_target_pairs={{0,4},{4,0},{8,12},{12,8},{16,20},{20,16},{24,28},{28,24},{1,5},{5... | collective-permute-start | bytes 589832 | tf_op jit(solution)/shard_map/ppermute | solution.py:12
  14.1 21.5 %collective-permute-start.2 = (bf16[4,96,256]{2,1,0:T(8,128)(2,1)S(1)}, bf16[4,96,256]{2,1,0:T(8,128)(2,1)S(1)}, u32[]{:S(2)}, u32[]{:S(2)}) collective-permute-start(bf16[4,96,256]{2,1,0:T(8,128)(2,1)S(1)} %get-tuple-element.14), channel_id=1, source_target_pairs={{0,12},{4,8},{8,4},{12,0},{16,28},{20,24},{24,20},{28,16},{1,13},{... | collective-permute-start | bytes 589832 | tf_op jit(solution)/shard_map/ppermute | solution.py:12
  17.0 20.2 %collective-permute-start.1 = (bf16[4,96,256]{2,1,0:T(8,128)(2,1)S(1)}, bf16[4,96,256]{2,1,0:T(8,128)(2,1)S(1)}, u32[]{:S(2)}, u32[]{:S(2)}) collective-permute-start(bf16[4,96,256]{2,1,0:T(8,128)(2,1)S(1)} %get-tuple-element.15), channel_id=1, source_target_pairs={{0,8},{4,12},{8,0},{12,4},{16,24},{20,28},{24,16},{28,20},{1,9},{5... | collective-permute-start | bytes 589832 | tf_op jit(solution)/shard_map/ppermute | solution.py:12
  19.5 18.0 %collective-permute-start = (bf16[4,96,256]{2,1,0:T(8,128)(2,1)S(1)}, bf16[4,96,256]{2,1,0:T(8,128)(2,1)S(1)}, u32[]{:S(2)}, u32[]{:S(2)}) collective-permute-start(bf16[4,96,256]{2,1,0:T(8,128)(2,1)S(1)} %get-tuple-element.13), channel_id=1, source_target_pairs={{0,4},{4,0},{8,12},{12,8},{16,20},{20,16},{24,28},{28,24},{1,5},{5... | collective-permute-start | bytes 589832 | tf_op jit(solution)/shard_map/ppermute | solution.py:12
  25.6 8.9 %collective-permute-start.21 = (bf16[4,64,256]{2,1,0:T(8,128)(2,1)S(1)}, bf16[4,64,256]{2,1,0:T(8,128)(2,1)S(1)}, u32[]{:S(2)}, u32[]{:S(2)}) collective-permute-start(bf16[4,64,256]{2,1,0:T(8,128)(2,1)S(1)} %fusion.23), channel_id=1, source_target_pairs={{0,16},{4,20},{8,24},{12,28},{16,0},{20,4},{24,8},{28,12},{1,17},{... | collective-permute-start | bytes 393224 | tf_op jit(solution)/shard_map/ppermute | solution.py:12
  28.0 17.1 %collective-permute-start.12 = (bf16[4,96,256]{2,1,0:T(8,128)(2,1)S(1)}, bf16[4,96,256]{2,1,0:T(8,128)(2,1)S(1)}, u32[]{:S(2)}, u32[]{:S(2)}) collective-permute-start(bf16[4,96,256]{2,1,0:T(8,128)(2,1)S(1)} %fusion.22), channel_id=1, source_target_pairs={{0,16},{4,20},{8,24},{12,28},{16,0},{20,4},{24,8},{28,12},{1,17},{... | collective-permute-start | bytes 589832 | tf_op jit(solution)/shard_map/ppermute | solution.py:12
  35.5 5.6 %collective-permute-start.22 = (bf16[64,256]{1,0:T(8,128)(2,1)S(1)}, bf16[64,256]{1,0:T(8,128)(2,1)S(1)}, u32[]{:S(2)}, u32[]{:S(2)}) collective-permute-start(bf16[64,256]{1,0:T(8,128)(2,1)S(1)} %get-tuple-element.59), channel_id=1, source_target_pairs={{0,1},{1,0},{2,3},{3,2},{4,5},{5,4},{6,7},{7,6},{8,9},{9,8},{10,11... | collective-permute-start | bytes 98312 | tf_op jit(solution)/shard_map/ppermute | solution.py:12
  35.6 5.5 %collective-permute-start.23 = (bf16[64,256]{1,0:T(8,128)(2,1)S(1)}, bf16[64,256]{1,0:T(8,128)(2,1)S(1)}, u32[]{:S(2)}, u32[]{:S(2)}) collective-permute-start(bf16[64,256]{1,0:T(8,128)(2,1)S(1)} %get-tuple-element.57), channel_id=1, source_target_pairs={{0,2},{1,3},{2,0},{3,1},{4,6},{5,7},{6,4},{7,5},{8,10},{9,11},{10,... | collective-permute-start | bytes 98312 | tf_op jit(solution)/shard_map/ppermute | solution.py:12
  37.2 3.9 %collective-permute-start.24 = (bf16[64,256]{1,0:T(8,128)(2,1)S(1)}, bf16[64,256]{1,0:T(8,128)(2,1)S(1)}, u32[]{:S(2)}, u32[]{:S(2)}) collective-permute-start(bf16[64,256]{1,0:T(8,128)(2,1)S(1)} %get-tuple-element.58), channel_id=1, source_target_pairs={{0,3},{1,2},{2,1},{3,0},{4,7},{5,6},{6,5},{7,4},{8,11},{9,10},{10,... | collective-permute-start | bytes 98312 | tf_op jit(solution)/shard_map/ppermute | solution.py:12
  37.6 13.1 %collective-permute-start.3 = (bf16[4,96,256]{2,1,0:T(8,128)(2,1)S(1)}, bf16[4,96,256]{2,1,0:T(8,128)(2,1)S(1)}, u32[]{:S(2)}, u32[]{:S(2)}) collective-permute-start(bf16[4,96,256]{2,1,0:T(8,128)(2,1)S(1)} %fusion.21), channel_id=1, source_target_pairs={{0,16},{4,20},{8,24},{12,28},{16,0},{20,4},{24,8},{28,12},{1,17},{... | collective-permute-start | bytes 589832 | tf_op jit(solution)/shard_map/ppermute | solution.py:12
  41.2 16.0 %collective-permute-start.25 = (bf16[1,64,1024]{2,1,0:T(8,128)(2,1)S(1)}, bf16[1,64,1024]{2,1,0:T(8,128)(2,1)S(1)}, u32[]{:S(2)}, u32[]{:S(2)}) collective-permute-start(bf16[1,64,1024]{2,1,0:T(8,128)(2,1)S(1)} %maximum_bitcast_fusion.2), channel_id=1, source_target_pairs={{0,8},{4,12},{8,0},{12,4},{16,24},{20,28},{24,16},{28,20},{1,9},{5... | collective-permute-start | bytes 393224 | tf_op jit(solution)/shard_map/ppermute | solution.py:12
  46.3 4.6 %collective-permute-start.13 = (bf16[96,256]{1,0:T(8,128)(2,1)S(1)}, bf16[96,256]{1,0:T(8,128)(2,1)S(1)}, u32[]{:S(2)}, u32[]{:S(2)}) collective-permute-start(bf16[96,256]{1,0:T(8,128)(2,1)S(1)} %get-tuple-element.56), channel_id=1, source_target_pairs={{0,1},{1,0},{2,3},{3,2},{4,5},{5,4},{6,7},{7,6},{8,9},{9,8},{10,11... | collective-permute-start | bytes 147464 | tf_op jit(solution)/shard_map/ppermute | solution.py:12
  46.4 6.1 %collective-permute-start.14 = (bf16[96,256]{1,0:T(8,128)(2,1)S(1)}, bf16[96,256]{1,0:T(8,128)(2,1)S(1)}, u32[]{:S(2)}, u32[]{:S(2)}) collective-permute-start(bf16[96,256]{1,0:T(8,128)(2,1)S(1)} %get-tuple-element.54), channel_id=1, source_target_pairs={{0,2},{1,3},{2,0},{3,1},{4,6},{5,7},{6,4},{7,5},{8,10},{9,11},{10,... | collective-permute-start | bytes 147464 | tf_op jit(solution)/shard_map/ppermute | solution.py:12
  48.0 4.9 %collective-permute-start.15 = (bf16[96,256]{1,0:T(8,128)(2,1)S(1)}, bf16[96,256]{1,0:T(8,128)(2,1)S(1)}, u32[]{:S(2)}, u32[]{:S(2)}) collective-permute-start(bf16[96,256]{1,0:T(8,128)(2,1)S(1)} %get-tuple-element.55), channel_id=1, source_target_pairs={{0,3},{1,2},{2,1},{3,0},{4,7},{5,6},{6,5},{7,4},{8,11},{9,10},{10,... | collective-permute-start | bytes 147464 | tf_op jit(solution)/shard_map/ppermute | solution.py:12
  50.9 2.9 %collective-permute-start.4 = (bf16[96,256]{1,0:T(8,128)(2,1)S(1)}, bf16[96,256]{1,0:T(8,128)(2,1)S(1)}, u32[]{:S(2)}, u32[]{:S(2)}) collective-permute-start(bf16[96,256]{1,0:T(8,128)(2,1)S(1)} %get-tuple-element.53), channel_id=1, source_target_pairs={{0,1},{1,0},{2,3},{3,2},{4,5},{5,4},{6,7},{7,6},{8,9},{9,8},{10,11... | collective-permute-start | bytes 147464 | tf_op jit(solution)/shard_map/ppermute | solution.py:12
  51.0 4.2 %collective-permute-start.5 = (bf16[96,256]{1,0:T(8,128)(2,1)S(1)}, bf16[96,256]{1,0:T(8,128)(2,1)S(1)}, u32[]{:S(2)}, u32[]{:S(2)}) collective-permute-start(bf16[96,256]{1,0:T(8,128)(2,1)S(1)} %get-tuple-element.51), channel_id=1, source_target_pairs={{0,2},{1,3},{2,0},{3,1},{4,6},{5,7},{6,4},{7,5},{8,10},{9,11},{10,... | collective-permute-start | bytes 147464 | tf_op jit(solution)/shard_map/ppermute | solution.py:12
  52.6 3.7 %collective-permute-start.6 = (bf16[96,256]{1,0:T(8,128)(2,1)S(1)}, bf16[96,256]{1,0:T(8,128)(2,1)S(1)}, u32[]{:S(2)}, u32[]{:S(2)}) collective-permute-start(bf16[96,256]{1,0:T(8,128)(2,1)S(1)} %get-tuple-element.52), channel_id=1, source_target_pairs={{0,3},{1,2},{2,1},{3,0},{4,7},{5,6},{6,5},{7,4},{8,11},{9,10},{10,... | collective-permute-start | bytes 147464 | tf_op jit(solution)/shard_map/ppermute | solution.py:12
  52.9 7.8 %collective-permute-start.16 = (bf16[1,96,1024]{2,1,0:T(8,128)(2,1)S(1)}, bf16[1,96,1024]{2,1,0:T(8,128)(2,1)S(1)}, u32[]{:S(2)}, u32[]{:S(2)}) collective-permute-start(bf16[1,96,1024]{2,1,0:T(8,128)(2,1)S(1)} %maximum_bitcast_fusion.1), channel_id=1, source_target_pairs={{0,8},{4,12},{8,0},{12,4},{16,24},{20,28},{24,16},{28,20},{1,9},{5... | collective-permute-start | bytes 589832 | tf_op jit(solution)/shard_map/ppermute | solution.py:12
  56.3 8.0 %collective-permute-start.7 = (bf16[1,96,1024]{2,1,0:T(8,128)(2,1)S(1)}, bf16[1,96,1024]{2,1,0:T(8,128)(2,1)S(1)}, u32[]{:S(2)}, u32[]{:S(2)}) collective-permute-start(bf16[1,96,1024]{2,1,0:T(8,128)(2,1)S(1)} %maximum_bitcast_fusion), channel_id=1, source_target_pairs={{0,8},{4,12},{8,0},{12,4},{16,24},{20,28},{24,16},{28,20},{1,9},{5... | collective-permute-start | bytes 589832 | tf_op jit(solution)/shard_map/ppermute | solution.py:12
  58.0 8.8 %collective-permute-start.26 = (bf16[2,64,1024]{2,1,0:T(8,128)(2,1)}, bf16[2,64,1024]{2,1,0:T(8,128)(2,1)}, u32[]{:S(2)}, u32[]{:S(2)}) collective-permute-start(bf16[2,64,1024]{2,1,0:T(8,128)(2,1)} %pad_maximum_fusion.3), channel_id=1, source_target_pairs={{0,4},{4,0},{8,12},{12,8},{16,20},{20,16},{24,28},{28,24},{1,5},{5... | collective-permute-start | bytes 786440 | tf_op jit(solution)/shard_map/ppermute | solution.py:12
  64.6 12.2 %collective-permute-start.17 = (bf16[2,96,1024]{2,1,0:T(8,128)(2,1)S(1)}, bf16[2,96,1024]{2,1,0:T(8,128)(2,1)}, u32[]{:S(2)}, u32[]{:S(2)}) collective-permute-start(bf16[2,96,1024]{2,1,0:T(8,128)(2,1)S(1)} %pad_maximum_fusion.2), channel_id=1, source_target_pairs={{0,4},{4,0},{8,12},{12,8},{16,20},{20,16},{24,28},{28,24},{1,5},{5... | collective-permute-start | bytes 1179656 | tf_op jit(solution)/shard_map/ppermute | solution.py:12
  66.1 17.9 %collective-permute-start.8 = (bf16[2,96,1024]{2,1,0:T(8,128)(2,1)S(1)}, bf16[2,96,1024]{2,1,0:T(8,128)(2,1)S(1)}, u32[]{:S(2)}, u32[]{:S(2)}) collective-permute-start(bf16[2,96,1024]{2,1,0:T(8,128)(2,1)S(1)} %pad_maximum_fusion.1), channel_id=1, source_target_pairs={{0,4},{4,0},{8,12},{12,8},{16,20},{20,16},{24,28},{28,24},{1,5},{5... | collective-permute-start | bytes 1179656 | tf_op jit(solution)/shard_map/ppermute | solution.py:12
  89.7 5.5 %copy-start.1 = (bf16[1024,1024]{1,0:T(8,128)(2,1)S(1)}, bf16[1024,1024]{1,0:T(8,128)(2,1)}, u32[]{:S(2)}) copy-start(bf16[1024,1024]{1,0:T(8,128)(2,1)} %pad_maximum_fusion) | copy-start | bytes 6291460
  89.8 6.7 %collective-permute-start.29 = (bf16[128,256]{1,0:T(8,128)(2,1)S(1)}, bf16[128,256]{1,0:T(8,128)(2,1)S(1)}, u32[]{:S(2)}, u32[]{:S(2)}) collective-permute-start(bf16[128,256]{1,0:T(8,128)(2,1)S(1)} %bitcast.164), channel_id=1, source_target_pairs={{0,3},{1,2},{2,1},{3,0},{4,7},{5,6},{6,5},{7,4},{8,11},{9,10},{10,... | collective-permute-start | bytes 196616 | tf_op jit(solution)/shard_map/ppermute | solution.py:12
  89.8 6.6 %collective-permute-start.28 = (bf16[128,256]{1,0:T(8,128)(2,1)S(1)}, bf16[128,256]{1,0:T(8,128)(2,1)S(1)}, u32[]{:S(2)}, u32[]{:S(2)}) collective-permute-start(bf16[128,256]{1,0:T(8,128)(2,1)S(1)} %bitcast.165), channel_id=1, source_target_pairs={{0,2},{1,3},{2,0},{3,1},{4,6},{5,7},{6,4},{7,5},{8,10},{9,11},{10,... | collective-permute-start | bytes 196616 | tf_op jit(solution)/shard_map/ppermute | solution.py:12
  91.2 5.2 %collective-permute-start.27 = (bf16[128,256]{1,0:T(8,128)(2,1)S(1)}, bf16[128,256]{1,0:T(8,128)(2,1)S(1)}, u32[]{:S(2)}, u32[]{:S(2)}) collective-permute-start(bf16[128,256]{1,0:T(8,128)(2,1)S(1)} %bitcast.166), channel_id=1, source_target_pairs={{0,1},{1,0},{2,3},{3,2},{4,5},{5,4},{6,7},{7,6},{8,9},{9,8},{10,11... | collective-permute-start | bytes 196616 | tf_op jit(solution)/shard_map/ppermute | solution.py:12
  (5 other events, 11.0 us)

commit v2 on v0

v2 whole, which is shorter than its diff:
```python
import functools

import jax
import jax.numpy as jnp
from jax import lax
from jax.experimental import pallas as pl
from jax.experimental.pallas import tpu as pltpu
from jax.sharding import PartitionSpec as P

stat_decay = 0.9
chunk_parts = (1,1,1,1)
sum_ways = (1,)
gather_ways = (1, -1,)
vmem_bytes = 24 * 2**20


def swap(values, axis, mask):
    size = lax.axis_size(axis)
    return lax.ppermute(values, axis, [(i, i ^ mask) for i in range(size)])


def pick(values, index, dim):
    return lax.dynamic_index_in_dim(values, index, dim, keepdims=False)


def ordered(pieces, index):
    count = len(pieces)
    return [
        lax.select_n(index, *[pieces[place ^ me] for me in range(count)])
        for place in range(count)
    ]


def chunks_of(rows):
    total = sum(chunk_parts)
    edges = [0]
    for part in chunk_parts:
        edges.append(edges[-1] + rows * part // total)
    return list(zip(edges[:-1], edges[1:]))


def wave(count, stages):
    return [
        (k, s)
        for turn in range(count * 1 + stages)
        for k in reversed(range(count))
        for s in range(stages)
        if k * 1 + s == turn
    ]


def update_kernel(count, blk_ref, *refs):
    strips, (root_rows, right_root), outs, rows = refs[:count], refs[count : count + 2], refs[count + 2 : -1], refs[-1]
    total = None
    start = 0
    for strip in strips:
        stop = start + strip.shape[0]
        part = jnp.dot(
            root_rows[0, :, start:stop], strip[...], preferred_element_type=jnp.float32
        )
        total = part if total is None else total + part
        start = stop
    rows[...] = jnp.dot(
        total.astype(jnp.bfloat16), right_root[0], preferred_element_type=jnp.float32
    ).astype(jnp.bfloat16)
    width = outs[0].shape[1]
    for m, out in enumerate(outs):
        out[...] = rows[:, pl.ds(pl.multiple_of((blk_ref[1] ^ m) * width, width), width)]


def make_update(blk_index, dp_index, strips, left_root, right_root, strip_rows, owners, cols):
    block_size = left_root.shape[-1]
    whole = lambda shape: pl.BlockSpec(shape, lambda i, s: (0,) * len(shape))
    return pl.pallas_call(
        functools.partial(update_kernel, len(strips)),
        grid_spec=pltpu.PrefetchScalarGridSpec(
            num_scalar_prefetch=1,
            grid=(1,),
            in_specs=[whole(s.shape) for s in strips]
            + [
                pl.BlockSpec((1, strip_rows, block_size), lambda i, s: (0, s[0], 0)),
                whole(right_root.shape),
            ],
            out_specs=[whole((strip_rows, cols))] * owners,
            scratch_shapes=[pltpu.VMEM((strip_rows, block_size), jnp.bfloat16)],
        ),
        out_shape=[jax.ShapeDtypeStruct((strip_rows, cols), jnp.bfloat16)] * owners,
        compiler_params=pltpu.CompilerParams(vmem_limit_bytes=vmem_bytes),
        cost_estimate=pl.CostEstimate(flops=1000, bytes_accessed=1000, transcendentals=0),
    )(jnp.stack([dp_index, blk_index]).astype(jnp.int32), *strips, left_root, right_root)


def stat_kernel(count, dp_ref, *refs):
    strips, (left_old, right_old, left_new, right_new, whole) = refs[:count], refs[count:]
    start = 0
    for strip in strips:
        whole[start : start + strip.shape[0], :] = strip[...]
        start += strip.shape[0]
    rows = left_old.shape[1]
    scale = (1.0 - stat_decay) / whole.shape[0]
    place = pl.ds(pl.multiple_of(dp_ref[0] * rows, rows), rows)
    left_prod = lax.dot_general(
        whole[place, :], whole[...], (((1,), (1,)), ((), ())), preferred_element_type=jnp.float32
    )
    left_new[0] = stat_decay * left_old[0] + scale * left_prod
    right_prod = lax.dot_general(
        whole[:, place], whole[...], (((0,), (0,)), ((), ())), preferred_element_type=jnp.float32
    )
    right_new[0] = stat_decay * right_old[0] + scale * right_prod


def make_stats(dp_index, strips, left_old, right_old):
    block_size = left_old.shape[-1]
    same = [jax.ShapeDtypeStruct(left_old.shape, jnp.float32)] * 2
    vmem = pl.BlockSpec(memory_space=pltpu.VMEM)
    return pl.pallas_call(
        functools.partial(stat_kernel, len(strips)),
        in_specs=[pl.BlockSpec(memory_space=pltpu.SMEM)] + [vmem] * (len(strips) + 2),
        out_specs=[vmem] * 2,
        out_shape=same,
        scratch_shapes=[pltpu.VMEM((block_size, block_size), jnp.bfloat16)],
        compiler_params=pltpu.CompilerParams(vmem_limit_bytes=vmem_bytes),
        cost_estimate=pl.CostEstimate(flops=1000, bytes_accessed=1000, transcendentals=0),
    )(dp_index.astype(jnp.int32)[None], *strips, left_old, right_old)


def on_device(grads, left_old, right_old, left_root, right_root):
    members, owners = lax.axis_size("dp"), lax.axis_size("blk")
    near = members // 2
    bits = near.bit_length() - 1
    block_size = left_root.shape[-1]
    strip_rows = left_old.shape[1]
    dp_index = lax.axis_index("dp")
    blk_index = lax.axis_index("blk")
    place = [(dp_index >> j) & 1 for j in range(bits)]
    cols = grads.shape[3]
    spans = chunks_of(block_size)
    state = {}
    last = [None]

    def after(values):
        if last[0] is None:
            return values
        return lax.optimization_barrier((values, last[0]))[0]

    def dim_of(j, taken):
        return 1 + len([i for i in range(bits) if i > j and i not in taken])

    def send(k, s, values):
        with jax.named_scope(f"R{s}c{k}m0"):
            return swap(values, "dp", 1 << rs_order(k)[s])

    def rs_order(k):
        return list(range(bits))[:: sum_ways[k % len(sum_ways)]]

    def ag_order(k):
        return list(range(bits))[:: gather_ways[k % len(gather_ways)]]

    def part_of(k, j, index):
        start, stop = spans[k]
        high, depth = 2 ** (bits - 1 - j), (stop - start) // near
        low = 2**j * depth
        rows = grads[0, :, start:stop].reshape(owners, high, 2, low, cols)
        rows = lax.dynamic_slice_in_dim(rows, index, 1, 2)
        return rows.reshape(owners, *([2] * (bits - 1)), depth, cols)

    def first(k):
        j = rs_order(k)[0]
        state[k] = send(k, 0, part_of(k, j, 1 - place[j]))

    def step(k, s):
        order = rs_order(k)
        if s < bits:
            if s == 0:
                own, received = part_of(k, order[0], place[order[0]]), after(state[k])
            else:
                own, received = state[k]
                received = after(received)
                own = pick(own, place[order[s]], dim_of(order[s], order[:s]))
            total = own.astype(jnp.float32) + received.astype(jnp.float32)
            if s + 1 < bits:
                j = order[s + 1]
                sent = pick(total, 1 - place[j], dim_of(j, order[: s + 1])).astype(jnp.bfloat16)
                state[k] = (total, send(k, s + 1, sent))
            else:
                sent = total.astype(jnp.bfloat16)
                with jax.named_scope(f"Z{k}m0"):
                    state[k] = (total, swap(sent, "dp", near))
            last[0] = sent
        elif s == bits:
            total, far = state[k]
            far = after(far)
            owned = (total + far.astype(jnp.float32)).astype(jnp.bfloat16)
            state[k] = [pick(owned, blk_index, 0)]
            for m in range(1, owners):
                with jax.named_scope(f"B{k}m{m}"):
                    state[k].append(swap(pick(owned, blk_index ^ m, 0), "blk", m))
            last[0] = owned
        else:
            g = s - bits - 1
            if g == 0:
                pieces = after(state[k])
                strip = jnp.concatenate(ordered(pieces, blk_index), axis=1)[None]
            else:
                strip, other = state[k]
                other = after(other)
                j = ag_order(k)[g - 1]
                strip = jnp.concatenate(ordered([strip, other], place[j]), axis=0)
            last[0] = strip
            if g < bits:
                with jax.named_scope(f"A{g}c{k}m0"):
                    state[k] = (strip, swap(strip, "dp", 1 << ag_order(k)[g]))
            else:
                state[k] = strip

    order = [] or wave(len(spans), 2 * bits + 2)
    for k in range(len(spans)):
        first(k)
    for k, s in order:
        step(k, s)
    strips = []
    for k in range(len(spans)):
        places = [0]
        for j in ag_order(k):
            places = places + [p + (1 << j) for p in places]
        strip = state[k]
        if places != list(range(near)):
            strip = jnp.concatenate([strip[places.index(p)][None] for p in range(near)], axis=0)
        strips.append(strip.reshape(-1, block_size))

    aligned = cols % 128 == 0 and strip_rows % 128 == 0
    if aligned:
        back = list(make_update(blk_index, dp_index, strips, left_root, right_root, strip_rows, owners, cols))
    else:
        whole = jnp.concatenate(strips, axis=0)
        root_rows = lax.dynamic_slice_in_dim(left_root[0], dp_index * strip_rows, strip_rows, 0)
        half_done = jnp.dot(root_rows, whole, preferred_element_type=jnp.float32)
        full = jnp.dot(
            half_done.astype(jnp.bfloat16), right_root[0], preferred_element_type=jnp.float32
        )
        by_columns = full.astype(jnp.bfloat16).reshape(strip_rows, owners, cols)
        back = [pick(by_columns, blk_index ^ m, 1) for m in range(owners)]
    for m in range(1, owners):
        with jax.named_scope(f"U0m{m}"):
            back[m] = swap(back[m], "blk", m)
    if aligned:
        left_stat, right_stat = make_stats(dp_index, strips, left_old, right_old)
    else:
        own_rows = lax.dynamic_slice_in_dim(whole, dp_index * strip_rows, strip_rows, 0)
        own_columns = lax.dynamic_slice_in_dim(whole, dp_index * strip_rows, strip_rows, 1)
        left_prod = jnp.einsum("ik,jk->ij", own_rows, whole, preferred_element_type=jnp.float32)
        right_prod = jnp.einsum("ki,kj->ij", own_columns, whole, preferred_element_type=jnp.float32)
        stat_scale = (1.0 - stat_decay) / block_size
        left_stat = stat_decay * left_old + stat_scale * left_prod
        right_stat = stat_decay * right_old + stat_scale * right_prod
    update = jnp.stack(ordered(back, blk_index))
    return (update, left_stat, right_stat)


def solution(mesh):
    placed = (
        P("dp", None, None, "blk"),
        P("blk", "dp", None),
        P("blk", "dp", None),
        P("blk", None, None),
        P("blk", None, None),
    )
    return jax.shard_map(
        on_device,
        mesh=mesh,
        in_specs=placed,
        out_specs=(P(None, "dp", "blk"), P("blk", "dp", None), P("blk", "dp", None)),
        check_vma=False,
    )
```

time: 192 us -> 81.3 us (0.42)
  waiting for transfers between devices: 143 us -> 28 us
  starting transfers between devices: 3.62 us -> 39.5 us
  between operations: 14.1 us -> 1.17 us
  blocking collectives: 9.1 us -> 0 us
  matrix products: 7.55 us -> 0 us
  Pallas kernels: 0 us -> 3.39 us
  local copies, waits for them, and re-layouts: 7.02 us -> 3.93 us
  other arithmetic: 7.29 us -> 5.07 us
    reduce_scatter x1 -> x0, waiting for transfers between devices: 91.3 us -> none  [on_device(): lax.psum_scatter(member_terms, 'dp', scatter_dimension=1, tiled=True)]
    all_gather x1 -> x0, waiting for transfers between devices: 50.1 us -> none  [on_device(): whole_block = lax.all_gather(owned_rows, 'dp', axis=1, tiled=True)]
    ppermute x0 -> x35, starting transfers between devices: none -> 39.5 us  [swap(): return lax.ppermute(values, axis, [(i, i ^ mask) for i in range(size)])]
    ppermute x0 -> x35, waiting for transfers between devices: none -> 28 us  [swap(): return lax.ppermute(values, axis, [(i, i ^ mask) for i in range(size)])]
    all_to_all x1 -> x0, blocking collectives: 9.1 us -> none  [on_device(): lax.all_to_all(fsdp_shard, 'blk', split_axis=0, concat_axis=2, tiled=True)]
    dot_general x3 -> x0, matrix products: 7.55 us -> none  [the longest x1 3.1 us: on_device(): jnp.einsum('bik,bjk->bij', owned_rows, whole_block, preferred_element_typ...]
    convert_element_type x2 -> x8, other arithmetic: 5.08 us -> 0.32 us  [the longest x4 0.2 us: step(): owned = (total + far.astype(jnp.float32)).astype(jnp.bfloat16)]
    unnamed x14 -> x8, local copies, waits for them, and re-layouts: 6.63 us -> 1.95 us
  transfers between devices with their start and end apart: 3 -> 35, of which waited for: 3 -> 14; matrix products, arithmetic and copies ran while one was open for 2% -> 5% of each run, Pallas kernels for 0% -> 2%
where the time goes in v2:
time: 81.3 us; the launch traced here: 81.1 us
  starting transfers between devices  39.5 us (49%)
  waiting for transfers between devices  28 us (34%)
  other arithmetic  5.07 us (6%)
  local copies, waits for them, and re-layouts  3.93 us (5%)
  Pallas kernels  3.39 us (4%)
  between operations  1.17 us (1%)
    ppermute x35, starting transfers between devices, swap(): return lax.ppermute(values, axis, [(i, i ^ mask) for i in range(size)])  39.5 us
    ppermute x35, waiting for transfers between devices, swap(): return lax.ppermute(values, axis, [(i, i ^ mask) for i in range(size)])  28 us
    add x4, other arithmetic, step(): total = own.astype(jnp.float32) + received.astype(jnp.float32)  3.08 us
    pallas_call x1, Pallas kernels, make_stats(): pl.pallas_call(functools.partial(stat_kernel, len(strips)), in_specs=[pl....  2 us
    unnamed x8, local copies, waits for them, and re-layouts  1.95 us
    slice x1, local copies, waits for them, and re-layouts, part_of(): rows = grads[0, :, start:stop].reshape(owners, high, 2, low, cols)  1.66 us
  transfers between devices with their start and end apart: 35, of which 14 were waited for; matrix products, arithmetic and copies ran while one was open for 5% of the time, Pallas kernels for 2%

profile of v2, /device:TPU:0, one launch (start us, length us, event | category | flops | bytes accessed | tf_op | source)
XLA Modules:
  0.0 81.1 jit_solution(7169290589984926540)
XLA Ops:
  0.6 1.7 %fusion.8 = (bf16[1,4,256,256]{3,2,1,0:T(8,128)(2,1)S(1)}, bf16[1,4,256,256]{3,2,1,0:T(8,128)(2,1)S(1)}, bf16[1,4,256,256]{3,2,1,0:T(8,128)(2,1)S(1)}, bf16[1,4,256,256]{3,2,1,0:T(8,128)(2,1)S(1)}) fusion(bf16[1,4,1024,256]{3,2,1,0:T(8,128)(2,1)} %param.5), kind=kLoop, calls=%fused_computation.94 | loop fusion | bytes 4194304 | tf_op jit(solution)/shard_map/slice | solution.py:163
  2.3 3.0 %collective-permute-start = (bf16[4,2,64,256]{3,2,1,0:T(8,128)(2,1)S(1)}, bf16[4,2,64,256]{3,2,1,0:T(8,128)(2,1)}, u32[]{:S(2)}, u32[]{:S(2)}) collective-permute-start(bf16[4,2,64,256]{3,2,1,0:T(8,128)(2,1)S(1)} %dynamic-slice_bitcast_fusion.3), channel_id=1, source_target_pairs={{0,4},{4,0},{8,12},{12,8},{16,20},{20,16},{24,28},{28,24},{1,5},{5... | collective-permute-start | bytes 786440 | tf_op jit(solution)/shard_map/R0c0m0/ppermute | solution.py:19
  5.5 2.1 %collective-permute-start.5 = (bf16[4,2,64,256]{3,2,1,0:T(8,128)(2,1)S(1)}, bf16[4,2,64,256]{3,2,1,0:T(8,128)(2,1)}, u32[]{:S(2)}, u32[]{:S(2)}) collective-permute-start(bf16[4,2,64,256]{3,2,1,0:T(8,128)(2,1)S(1)} %dynamic-slice_bitcast_fusion.1), channel_id=1, source_target_pairs={{0,4},{4,0},{8,12},{12,8},{16,20},{20,16},{24,28},{28,24},{1,5},{5... | collective-permute-start | bytes 786440 | tf_op jit(solution)/shard_map/R0c2m0/ppermute | solution.py:19
  7.8 4.8 %collective-permute-done = bf16[4,2,64,256]{3,2,1,0:T(8,128)(2,1)} collective-permute-done((bf16[4,2,64,256]{3,2,1,0:T(8,128)(2,1)S(1)}, bf16[4,2,64,256]{3,2,1,0:T(8,128)(2,1)}, u32[]{:S(2)}, u32[]{:S(2)}) %collective-permute-start) | collective-permute-done | bytes 262176 | tf_op jit(solution)/shard_map/R0c0m0/ppermute | solution.py:19
  13.7 2.2 %collective-permute-start.1 = (bf16[4,64,256]{2,1,0:T(8,128)(2,1)S(1)}, bf16[4,64,256]{2,1,0:T(8,128)(2,1)S(1)}, u32[]{:S(2)}, u32[]{:S(2)}) collective-permute-start(bf16[4,64,256]{2,1,0:T(8,128)(2,1)S(1)} %fusion.4), channel_id=1, source_target_pairs={{0,8},{4,12},{8,0},{12,4},{16,24},{20,28},{24,16},{28,20},{1,9},{5... | collective-permute-start | bytes 393224 | tf_op jit(solution)/shard_map/R1c0m0/ppermute | solution.py:19
  15.8 2.4 %collective-permute-done.2 = bf16[4,2,64,256]{3,2,1,0:T(8,128)(2,1)} collective-permute-done((bf16[4,2,64,256]{3,2,1,0:T(8,128)(2,1)S(1)}, bf16[4,2,64,256]{3,2,1,0:T(8,128)(2,1)}, u32[]{:S(2)}, u32[]{:S(2)}) %collective-permute-start.2) | collective-permute-done | bytes 262176 | tf_op jit(solution)/shard_map/R0c1m0/ppermute | solution.py:19
  19.3 2.2 %collective-permute-start.4 = (bf16[4,64,256]{2,1,0:T(8,128)(2,1)S(1)}, bf16[4,64,256]{2,1,0:T(8,128)(2,1)S(1)}, u32[]{:S(2)}, u32[]{:S(2)}) collective-permute-start(bf16[4,64,256]{2,1,0:T(8,128)(2,1)S(1)} %fusion.5), channel_id=1, source_target_pairs={{0,8},{4,12},{8,0},{12,4},{16,24},{20,28},{24,16},{28,20},{1,9},{5... | collective-permute-start | bytes 393224 | tf_op jit(solution)/shard_map/R1c1m0/ppermute | solution.py:19
  21.5 2.7 %collective-permute-start.3 = (bf16[4,64,256]{2,1,0:T(8,128)(2,1)S(1)}, bf16[4,64,256]{2,1,0:T(8,128)(2,1)S(1)}, u32[]{:S(2)}, u32[]{:S(2)}) collective-permute-start(bf16[4,64,256]{2,1,0:T(8,128)(2,1)S(1)} %fusion), channel_id=1, source_target_pairs={{0,16},{4,20},{8,24},{12,28},{16,0},{20,4},{24,8},{28,12},{1,17},{... | collective-permute-start | bytes 393224 | tf_op jit(solution)/shard_map/Z0m0/ppermute | solution.py:19
  25.2 1.9 %collective-permute-start.10 = (bf16[4,64,256]{2,1,0:T(8,128)(2,1)S(1)}, bf16[4,64,256]{2,1,0:T(8,128)(2,1)S(1)}, u32[]{:S(2)}, u32[]{:S(2)}) collective-permute-start(bf16[4,64,256]{2,1,0:T(8,128)(2,1)S(1)} %fusion.6), channel_id=1, source_target_pairs={{0,8},{4,12},{8,0},{12,4},{16,24},{20,28},{24,16},{28,20},{1,9},{5... | collective-permute-start | bytes 393224 | tf_op jit(solution)/shard_map/R1c2m0/ppermute | solution.py:19
  27.1 2.7 %collective-permute-start.9 = (bf16[4,64,256]{2,1,0:T(8,128)(2,1)S(1)}, bf16[4,64,256]{2,1,0:T(8,128)(2,1)S(1)}, u32[]{:S(2)}, u32[]{:S(2)}) collective-permute-start(bf16[4,64,256]{2,1,0:T(8,128)(2,1)S(1)} %fusion.1), channel_id=1, source_target_pairs={{0,16},{4,20},{8,24},{12,28},{16,0},{20,4},{24,8},{28,12},{1,17},{... | collective-permute-start | bytes 393224 | tf_op jit(solution)/shard_map/Z1m0/ppermute | solution.py:19
  29.9 1.6 %collective-permute-start.7 = (bf16[64,256]{1,0:T(8,128)(2,1)S(1)}, bf16[64,256]{1,0:T(8,128)(2,1)S(1)}, u32[]{:S(2)}, u32[]{:S(2)}) collective-permute-start(bf16[64,256]{1,0:T(8,128)(2,1)S(1)} %get-tuple-element.144), channel_id=1, source_target_pairs={{0,2},{1,3},{2,0},{3,1},{4,6},{5,7},{6,4},{7,5},{8,10},{9,11},{10,... | collective-permute-start | bytes 98312 | tf_op jit(solution)/shard_map/B0m2/ppermute | solution.py:19
  33.1 1.3 %collective-permute-done.9 = bf16[4,64,256]{2,1,0:T(8,128)(2,1)S(1)} collective-permute-done((bf16[4,64,256]{2,1,0:T(8,128)(2,1)S(1)}, bf16[4,64,256]{2,1,0:T(8,128)(2,1)S(1)}, u32[]{:S(2)}, u32[]{:S(2)}) %collective-permute-start.9) | collective-permute-done | bytes 131104 | tf_op jit(solution)/shard_map/Z1m0/ppermute | solution.py:19
  34.4 1.6 %collective-permute-start.16 = (bf16[4,64,256]{2,1,0:T(8,128)(2,1)S(1)}, bf16[4,64,256]{2,1,0:T(8,128)(2,1)S(1)}, u32[]{:S(2)}, u32[]{:S(2)}) collective-permute-start(bf16[4,64,256]{2,1,0:T(8,128)(2,1)S(1)} %fusion.2), channel_id=1, source_target_pairs={{0,16},{4,20},{8,24},{12,28},{16,0},{20,4},{24,8},{28,12},{1,17},{... | collective-permute-start | bytes 393224 | tf_op jit(solution)/shard_map/Z2m0/ppermute | solution.py:19
  36.2 1.6 %collective-permute-start.14 = (bf16[64,256]{1,0:T(8,128)(2,1)S(1)}, bf16[64,256]{1,0:T(8,128)(2,1)S(1)}, u32[]{:S(2)}, u32[]{:S(2)}) collective-permute-start(bf16[64,256]{1,0:T(8,128)(2,1)S(1)} %get-tuple-element.136), channel_id=1, source_target_pairs={{0,2},{1,3},{2,0},{3,1},{4,6},{5,7},{6,4},{7,5},{8,10},{9,11},{10,... | collective-permute-start | bytes 98312 | tf_op jit(solution)/shard_map/B1m2/ppermute | solution.py:19
  39.3 1.5 %collective-permute-start.12 = (bf16[1,64,1024]{2,1,0:T(8,128)(2,1)S(1)}, bf16[1,64,1024]{2,1,0:T(8,128)(2,1)S(1)}, u32[]{:S(2)}, u32[]{:S(2)}) collective-permute-start(bf16[1,64,1024]{2,1,0:T(8,128)(2,1)S(1)} %maximum_bitcast_fusion), channel_id=1, source_target_pairs={{0,4},{4,0},{8,12},{12,8},{16,20},{20,16},{24,28},{28,24},{1,5},{5... | collective-permute-start | bytes 393224 | tf_op jit(solution)/shard_map/A0c0m0/ppermute | solution.py:19
  40.9 1.8 %collective-permute-done.16 = bf16[4,64,256]{2,1,0:T(8,128)(2,1)S(1)} collective-permute-done((bf16[4,64,256]{2,1,0:T(8,128)(2,1)S(1)}, bf16[4,64,256]{2,1,0:T(8,128)(2,1)S(1)}, u32[]{:S(2)}, u32[]{:S(2)}) %collective-permute-start.16) | collective-permute-done | bytes 131104 | tf_op jit(solution)/shard_map/Z2m0/ppermute | solution.py:19
  42.9 2.6 %collective-permute-start.19 = (bf16[1,64,1024]{2,1,0:T(8,128)(2,1)S(1)}, bf16[1,64,1024]{2,1,0:T(8,128)(2,1)S(1)}, u32[]{:S(2)}, u32[]{:S(2)}) collective-permute-start(bf16[1,64,1024]{2,1,0:T(8,128)(2,1)S(1)} %maximum_bitcast_fusion.1), channel_id=1, source_target_pairs={{0,8},{4,12},{8,0},{12,4},{16,24},{20,28},{24,16},{28,20},{1,9},{5... | collective-permute-start | bytes 393224 | tf_op jit(solution)/shard_map/A0c1m0/ppermute | solution.py:19
  45.6 1.6 %collective-permute-start.21 = (bf16[64,256]{1,0:T(8,128)(2,1)S(1)}, bf16[64,256]{1,0:T(8,128)(2,1)S(1)}, u32[]{:S(2)}, u32[]{:S(2)}) collective-permute-start(bf16[64,256]{1,0:T(8,128)(2,1)S(1)} %get-tuple-element.128), channel_id=1, source_target_pairs={{0,2},{1,3},{2,0},{3,1},{4,6},{5,7},{6,4},{7,5},{8,10},{9,11},{10,... | collective-permute-start | bytes 98312 | tf_op jit(solution)/shard_map/B2m2/ppermute | solution.py:19
  47.5 2.1 %collective-permute-done.23 = bf16[4,64,256]{2,1,0:T(8,128)(2,1)S(1)} collective-permute-done((bf16[4,64,256]{2,1,0:T(8,128)(2,1)S(1)}, bf16[4,64,256]{2,1,0:T(8,128)(2,1)S(1)}, u32[]{:S(2)}, u32[]{:S(2)}) %collective-permute-start.23) | collective-permute-done | bytes 131104 | tf_op jit(solution)/shard_map/Z3m0/ppermute | solution.py:19
  50.5 1.6 %collective-permute-start.25 = (bf16[1,64,1024]{2,1,0:T(8,128)(2,1)S(1)}, bf16[1,64,1024]{2,1,0:T(8,128)(2,1)S(1)}, u32[]{:S(2)}, u32[]{:S(2)}) collective-permute-start(bf16[1,64,1024]{2,1,0:T(8,128)(2,1)S(1)} %maximum_bitcast_fusion.2), channel_id=1, source_target_pairs={{0,4},{4,0},{8,12},{12,8},{16,20},{20,16},{24,28},{28,24},{1,5},{5... | collective-permute-start | bytes 393224 | tf_op jit(solution)/shard_map/A0c2m0/ppermute | solution.py:19
  54.2 2.0 %collective-permute-done.18 = bf16[2,64,1024]{2,1,0:T(8,128)(2,1)S(1)} collective-permute-done((bf16[2,64,1024]{2,1,0:T(8,128)(2,1)S(1)}, bf16[2,64,1024]{2,1,0:T(8,128)(2,1)S(1)}, u32[]{:S(2)}, u32[]{:S(2)}) %collective-permute-start.18) | collective-permute-done | bytes 262176 | tf_op jit(solution)/shard_map/A1c0m0/ppermute | solution.py:19
  56.2 1.5 %collective-permute-start.24 = (bf16[2,64,1024]{2,1,0:T(8,128)(2,1)S(1)}, bf16[2,64,1024]{2,1,0:T(8,128)(2,1)S(1)}, u32[]{:S(2)}, u32[]{:S(2)}) collective-permute-start(bf16[2,64,1024]{2,1,0:T(8,128)(2,1)S(1)} %pad_maximum_fusion.5), channel_id=1, source_target_pairs={{0,4},{4,0},{8,12},{12,8},{16,20},{20,16},{24,28},{28,24},{1,5},{5... | collective-permute-start | bytes 786440 | tf_op jit(solution)/shard_map/A1c1m0/ppermute | solution.py:19
  58.7 1.5 %collective-permute-start.29 = (bf16[2,64,1024]{2,1,0:T(8,128)(2,1)S(1)}, bf16[2,64,1024]{2,1,0:T(8,128)(2,1)S(1)}, u32[]{:S(2)}, u32[]{:S(2)}) collective-permute-start(bf16[2,64,1024]{2,1,0:T(8,128)(2,1)S(1)} %pad_maximum_fusion.6), channel_id=1, source_target_pairs={{0,8},{4,12},{8,0},{12,4},{16,24},{20,28},{24,16},{28,20},{1,9},{5... | collective-permute-start | bytes 786440 | tf_op jit(solution)/shard_map/A1c2m0/ppermute | solution.py:19
  60.1 2.7 %collective-permute-done.24 = bf16[2,64,1024]{2,1,0:T(8,128)(2,1)S(1)} collective-permute-done((bf16[2,64,1024]{2,1,0:T(8,128)(2,1)S(1)}, bf16[2,64,1024]{2,1,0:T(8,128)(2,1)S(1)}, u32[]{:S(2)}, u32[]{:S(2)}) %collective-permute-start.24) | collective-permute-done | bytes 262176 | tf_op jit(solution)/shard_map/A1c1m0/ppermute | solution.py:19
  62.8 1.5 %collective-permute-done.30 = bf16[1,64,1024]{2,1,0:T(8,128)(2,1)S(1)} collective-permute-done((bf16[1,64,1024]{2,1,0:T(8,128)(2,1)S(1)}, bf16[1,64,1024]{2,1,0:T(8,128)(2,1)S(1)}, u32[]{:S(2)}, u32[]{:S(2)}) %collective-permute-start.30) | collective-permute-done | bytes 131104 | tf_op jit(solution)/shard_map/A0c3m0/ppermute | solution.py:19
  65.0 3.3 %collective-permute-done.29 = bf16[2,64,1024]{2,1,0:T(8,128)(2,1)S(1)} collective-permute-done((bf16[2,64,1024]{2,1,0:T(8,128)(2,1)S(1)}, bf16[2,64,1024]{2,1,0:T(8,128)(2,1)S(1)}, u32[]{:S(2)}, u32[]{:S(2)}) %collective-permute-start.29) | collective-permute-done | bytes 262176 | tf_op jit(solution)/shard_map/A1c2m0/ppermute | solution.py:19
  68.3 2.5 %collective-permute-done.31 = bf16[2,64,1024]{2,1,0:T(8,128)(2,1)S(1)} collective-permute-done((bf16[2,64,1024]{2,1,0:T(8,128)(2,1)S(1)}, bf16[2,64,1024]{2,1,0:T(8,128)(2,1)S(1)}, u32[]{:S(2)}, u32[]{:S(2)}) %collective-permute-start.31) | collective-permute-done | bytes 262176 | tf_op jit(solution)/shard_map/A1c3m0/ppermute | solution.py:19
  71.2 1.3 %copy-done = bf16[1,1024,1024]{2,1,0:T(8,128)(2,1)S(1)} copy-done((bf16[1,1024,1024]{2,1,0:T(8,128)(2,1)S(1)}, bf16[1,1024,1024]{2,1,0:T(8,128)(2,1)}, u32[]{:S(2)}) %copy-start) | copy-done | bytes 2097176
  73.1 1.4 %shard_map.76 = (bf16[128,256]{1,0:T(8,128)(2,1)S(1)}, bf16[128,256]{1,0:T(8,128)(2,1)S(1)}, bf16[128,256]{1,0:T(8,128)(2,1)S(1)}, bf16[128,256]{1,0:T(8,128)(2,1)S(1)}) custom-call(s32[2]{0:T(128)S(1)} %pad_add_fusion.blk_ref, bf16[256,1024]{1,0:T(8,128)(2,1)S(1)} %bitcast.126, bf16[256,1024]{1,0:T(8,128)(2,1)S(1)} %bitcast.130, ...), custom_call_target="tpu_custom_call" | custom-call | flops 1000 | bytes 1000 | tf_op jit(solution)/shard_map/pallas_call | solution.py:74
  74.5 1.5 %collective-permute-start.33 = (bf16[128,256]{1,0:T(8,128)(2,1)S(1)}, bf16[128,256]{1,0:T(8,128)(2,1)S(1)}, u32[]{:S(2)}, u32[]{:S(2)}) collective-permute-start(bf16[128,256]{1,0:T(8,128)(2,1)S(1)} %get-tuple-element.79), channel_id=1, source_target_pairs={{0,2},{1,3},{2,0},{3,1},{4,6},{5,7},{6,4},{7,5},{8,10},{9,11},{10,... | collective-permute-start | bytes 196616 | tf_op jit(solution)/shard_map/U0m2/ppermute | solution.py:19
  76.7 2.0 %shard_map.77 = (f32[1,128,1024]{2,1,0:T(8,128)}, f32[1,128,1024]{2,1,0:T(8,128)}) custom-call(s32[1]{0:T(128)} %bitcast.dp_ref, bf16[256,1024]{1,0:T(8,128)(2,1)S(1)} %bitcast.127, bf16[256,1024]{1,0:T(8,128)(2,1)S(1)} %bitcast.131, bf16[256,1024]{1,0:T(8,128)(2,1)S(1)} %bitcast.129, bf16[256,1024]{1,0:T(8,128)(2,1)S(1)} %bitcast.133, ...), custom_call_target="tpu_custom_call" | custom-call | flops 1000 | bytes 1000 | tf_op jit(solution)/shard_map/pallas_call | solution.py:116
  78.9 1.4 %collective-permute-done.34 = bf16[128,256]{1,0:T(8,128)(2,1)S(1)} collective-permute-done((bf16[128,256]{1,0:T(8,128)(2,1)S(1)}, bf16[128,256]{1,0:T(8,128)(2,1)S(1)}, u32[]{:S(2)}, u32[]{:S(2)}) %collective-permute-start.34) | collective-permute-done | bytes 65568 | tf_op jit(solution)/shard_map/U0m3/ppermute | solution.py:19
  (103 shorter events, 14.6 us)
Async XLA Ops:
  2.3 10.3 %collective-permute-start = (bf16[4,2,64,256]{3,2,1,0:T(8,128)(2,1)S(1)}, bf16[4,2,64,256]{3,2,1,0:T(8,128)(2,1)}, u32[]{:S(2)}, u32[]{:S(2)}) collective-permute-start(bf16[4,2,64,256]{3,2,1,0:T(8,128)(2,1)S(1)} %dynamic-slice_bitcast_fusion.3), channel_id=1, source_target_pairs={{0,4},{4,0},{8,12},{12,8},{16,20},{20,16},{24,28},{28,24},{1,5},{5... | collective-permute-start | bytes 786440 | tf_op jit(solution)/shard_map/R0c0m0/ppermute | solution.py:19
  5.4 12.8 %collective-permute-start.2 = (bf16[4,2,64,256]{3,2,1,0:T(8,128)(2,1)S(1)}, bf16[4,2,64,256]{3,2,1,0:T(8,128)(2,1)}, u32[]{:S(2)}, u32[]{:S(2)}) collective-permute-start(bf16[4,2,64,256]{3,2,1,0:T(8,128)(2,1)S(1)} %dynamic-slice_bitcast_fusion.2), channel_id=1, source_target_pairs={{0,4},{4,0},{8,12},{12,8},{16,20},{20,16},{24,28},{28,24},{1,5},{5... | collective-permute-start | bytes 786440 | tf_op jit(solution)/shard_map/R0c1m0/ppermute | solution.py:19
  5.5 18.6 %collective-permute-start.5 = (bf16[4,2,64,256]{3,2,1,0:T(8,128)(2,1)S(1)}, bf16[4,2,64,256]{3,2,1,0:T(8,128)(2,1)}, u32[]{:S(2)}, u32[]{:S(2)}) collective-permute-start(bf16[4,2,64,256]{3,2,1,0:T(8,128)(2,1)S(1)} %dynamic-slice_bitcast_fusion.1), channel_id=1, source_target_pairs={{0,4},{4,0},{8,12},{12,8},{16,20},{20,16},{24,28},{28,24},{1,5},{5... | collective-permute-start | bytes 786440 | tf_op jit(solution)/shard_map/R0c2m0/ppermute | solution.py:19
  7.6 23.9 %collective-permute-start.11 = (bf16[4,2,64,256]{3,2,1,0:T(8,128)(2,1)S(1)}, bf16[4,2,64,256]{3,2,1,0:T(8,128)(2,1)S(1)}, u32[]{:S(2)}, u32[]{:S(2)}) collective-permute-start(bf16[4,2,64,256]{3,2,1,0:T(8,128)(2,1)S(1)} %dynamic-slice_bitcast_fusion), channel_id=1, source_target_pairs={{0,4},{4,0},{8,12},{12,8},{16,20},{20,16},{24,28},{28,24},{1,5},{5... | collective-permute-start | bytes 786440 | tf_op jit(solution)/shard_map/R0c3m0/ppermute | solution.py:19
  13.7 7.8 %collective-permute-start.1 = (bf16[4,64,256]{2,1,0:T(8,128)(2,1)S(1)}, bf16[4,64,256]{2,1,0:T(8,128)(2,1)S(1)}, u32[]{:S(2)}, u32[]{:S(2)}) collective-permute-start(bf16[4,64,256]{2,1,0:T(8,128)(2,1)S(1)} %fusion.4), channel_id=1, source_target_pairs={{0,8},{4,12},{8,0},{12,4},{16,24},{20,28},{24,16},{28,20},{1,9},{5... | collective-permute-start | bytes 393224 | tf_op jit(solution)/shard_map/R1c0m0/ppermute | solution.py:19
  19.3 7.8 %collective-permute-start.4 = (bf16[4,64,256]{2,1,0:T(8,128)(2,1)S(1)}, bf16[4,64,256]{2,1,0:T(8,128)(2,1)S(1)}, u32[]{:S(2)}, u32[]{:S(2)}) collective-permute-start(bf16[4,64,256]{2,1,0:T(8,128)(2,1)S(1)} %fusion.5), channel_id=1, source_target_pairs={{0,8},{4,12},{8,0},{12,4},{16,24},{20,28},{24,16},{28,20},{1,9},{5... | collective-permute-start | bytes 393224 | tf_op jit(solution)/shard_map/R1c1m0/ppermute | solution.py:19
  21.5 8.3 %collective-permute-start.3 = (bf16[4,64,256]{2,1,0:T(8,128)(2,1)S(1)}, bf16[4,64,256]{2,1,0:T(8,128)(2,1)S(1)}, u32[]{:S(2)}, u32[]{:S(2)}) collective-permute-start(bf16[4,64,256]{2,1,0:T(8,128)(2,1)S(1)} %fusion), channel_id=1, source_target_pairs={{0,16},{4,20},{8,24},{12,28},{16,0},{20,4},{24,8},{28,12},{1,17},{... | collective-permute-start | bytes 393224 | tf_op jit(solution)/shard_map/Z0m0/ppermute | solution.py:19
  25.2 6.7 %collective-permute-start.10 = (bf16[4,64,256]{2,1,0:T(8,128)(2,1)S(1)}, bf16[4,64,256]{2,1,0:T(8,128)(2,1)S(1)}, u32[]{:S(2)}, u32[]{:S(2)}) collective-permute-start(bf16[4,64,256]{2,1,0:T(8,128)(2,1)S(1)} %fusion.6), channel_id=1, source_target_pairs={{0,8},{4,12},{8,0},{12,4},{16,24},{20,28},{24,16},{28,20},{1,9},{5... | collective-permute-start | bytes 393224 | tf_op jit(solution)/shard_map/R1c2m0/ppermute | solution.py:19
  27.1 7.3 %collective-permute-start.9 = (bf16[4,64,256]{2,1,0:T(8,128)(2,1)S(1)}, bf16[4,64,256]{2,1,0:T(8,128)(2,1)S(1)}, u32[]{:S(2)}, u32[]{:S(2)}) collective-permute-start(bf16[4,64,256]{2,1,0:T(8,128)(2,1)S(1)} %fusion.1), channel_id=1, source_target_pairs={{0,16},{4,20},{8,24},{12,28},{16,0},{20,4},{24,8},{28,12},{1,17},{... | collective-permute-start | bytes 393224 | tf_op jit(solution)/shard_map/Z1m0/ppermute | solution.py:19
  29.8 6.3 %collective-permute-start.6 = (bf16[64,256]{1,0:T(8,128)(2,1)S(1)}, bf16[64,256]{1,0:T(8,128)(2,1)S(1)}, u32[]{:S(2)}, u32[]{:S(2)}) collective-permute-start(bf16[64,256]{1,0:T(8,128)(2,1)S(1)} %get-tuple-element.145), channel_id=1, source_target_pairs={{0,1},{1,0},{2,3},{3,2},{4,5},{5,4},{6,7},{7,6},{8,9},{9,8},{10,11... | collective-permute-start | bytes 98312 | tf_op jit(solution)/shard_map/B0m1/ppermute | solution.py:19
  29.9 6.3 %collective-permute-start.7 = (bf16[64,256]{1,0:T(8,128)(2,1)S(1)}, bf16[64,256]{1,0:T(8,128)(2,1)S(1)}, u32[]{:S(2)}, u32[]{:S(2)}) collective-permute-start(bf16[64,256]{1,0:T(8,128)(2,1)S(1)} %get-tuple-element.144), channel_id=1, source_target_pairs={{0,2},{1,3},{2,0},{3,1},{4,6},{5,7},{6,4},{7,5},{8,10},{9,11},{10,... | collective-permute-start | bytes 98312 | tf_op jit(solution)/shard_map/B0m2/ppermute | solution.py:19
  31.5 6.3 %collective-permute-start.8 = (bf16[64,256]{1,0:T(8,128)(2,1)S(1)}, bf16[64,256]{1,0:T(8,128)(2,1)S(1)}, u32[]{:S(2)}, u32[]{:S(2)}) collective-permute-start(bf16[64,256]{1,0:T(8,128)(2,1)S(1)} %get-tuple-element.143), channel_id=1, source_target_pairs={{0,3},{1,2},{2,1},{3,0},{4,7},{5,6},{6,5},{7,4},{8,11},{9,10},{10,... | collective-permute-start | bytes 98312 | tf_op jit(solution)/shard_map/B0m3/ppermute | solution.py:19
  31.9 7.4 %collective-permute-start.17 = (bf16[4,64,256]{2,1,0:T(8,128)(2,1)S(1)}, bf16[4,64,256]{2,1,0:T(8,128)(2,1)S(1)}, u32[]{:S(2)}, u32[]{:S(2)}) collective-permute-start(bf16[4,64,256]{2,1,0:T(8,128)(2,1)S(1)} %fusion.7), channel_id=1, source_target_pairs={{0,8},{4,12},{8,0},{12,4},{16,24},{20,28},{24,16},{28,20},{1,9},{5... | collective-permute-start | bytes 393224 | tf_op jit(solution)/shard_map/R1c3m0/ppermute | solution.py:19
  34.4 8.3 %collective-permute-start.16 = (bf16[4,64,256]{2,1,0:T(8,128)(2,1)S(1)}, bf16[4,64,256]{2,1,0:T(8,128)(2,1)S(1)}, u32[]{:S(2)}, u32[]{:S(2)}) collective-permute-start(bf16[4,64,256]{2,1,0:T(8,128)(2,1)S(1)} %fusion.2), channel_id=1, source_target_pairs={{0,16},{4,20},{8,24},{12,28},{16,0},{20,4},{24,8},{28,12},{1,17},{... | collective-permute-start | bytes 393224 | tf_op jit(solution)/shard_map/Z2m0/ppermute | solution.py:19
  36.1 6.7 %collective-permute-start.13 = (bf16[64,256]{1,0:T(8,128)(2,1)S(1)}, bf16[64,256]{1,0:T(8,128)(2,1)S(1)}, u32[]{:S(2)}, u32[]{:S(2)}) collective-permute-start(bf16[64,256]{1,0:T(8,128)(2,1)S(1)} %get-tuple-element.137), channel_id=1, source_target_pairs={{0,1},{1,0},{2,3},{3,2},{4,5},{5,4},{6,7},{7,6},{8,9},{9,8},{10,11... | collective-permute-start | bytes 98312 | tf_op jit(solution)/shard_map/B1m1/ppermute | solution.py:19
  36.2 6.6 %collective-permute-start.14 = (bf16[64,256]{1,0:T(8,128)(2,1)S(1)}, bf16[64,256]{1,0:T(8,128)(2,1)S(1)}, u32[]{:S(2)}, u32[]{:S(2)}) collective-permute-start(bf16[64,256]{1,0:T(8,128)(2,1)S(1)} %get-tuple-element.136), channel_id=1, source_target_pairs={{0,2},{1,3},{2,0},{3,1},{4,6},{5,7},{6,4},{7,5},{8,10},{9,11},{10,... | collective-permute-start | bytes 98312 | tf_op jit(solution)/shard_map/B1m2/ppermute | solution.py:19
  37.8 5.1 %collective-permute-start.15 = (bf16[64,256]{1,0:T(8,128)(2,1)S(1)}, bf16[64,256]{1,0:T(8,128)(2,1)S(1)}, u32[]{:S(2)}, u32[]{:S(2)}) collective-permute-start(bf16[64,256]{1,0:T(8,128)(2,1)S(1)} %get-tuple-element.135), channel_id=1, source_target_pairs={{0,3},{1,2},{2,1},{3,0},{4,7},{5,6},{6,5},{7,4},{8,11},{9,10},{10,... | collective-permute-start | bytes 98312 | tf_op jit(solution)/shard_map/B1m3/ppermute | solution.py:19
  39.3 7.8 %collective-permute-start.12 = (bf16[1,64,1024]{2,1,0:T(8,128)(2,1)S(1)}, bf16[1,64,1024]{2,1,0:T(8,128)(2,1)S(1)}, u32[]{:S(2)}, u32[]{:S(2)}) collective-permute-start(bf16[1,64,1024]{2,1,0:T(8,128)(2,1)S(1)} %maximum_bitcast_fusion), channel_id=1, source_target_pairs={{0,4},{4,0},{8,12},{12,8},{16,20},{20,16},{24,28},{28,24},{1,5},{5... | collective-permute-start | bytes 393224 | tf_op jit(solution)/shard_map/A0c0m0/ppermute | solution.py:19
  42.7 6.9 %collective-permute-start.23 = (bf16[4,64,256]{2,1,0:T(8,128)(2,1)S(1)}, bf16[4,64,256]{2,1,0:T(8,128)(2,1)S(1)}, u32[]{:S(2)}, u32[]{:S(2)}) collective-permute-start(bf16[4,64,256]{2,1,0:T(8,128)(2,1)S(1)} %fusion.3), channel_id=1, source_target_pairs={{0,16},{4,20},{8,24},{12,28},{16,0},{20,4},{24,8},{28,12},{1,17},{... | collective-permute-start | bytes 393224 | tf_op jit(solution)/shard_map/Z3m0/ppermute | solution.py:19
  42.9 9.3 %collective-permute-start.19 = (bf16[1,64,1024]{2,1,0:T(8,128)(2,1)S(1)}, bf16[1,64,1024]{2,1,0:T(8,128)(2,1)S(1)}, u32[]{:S(2)}, u32[]{:S(2)}) collective-permute-start(bf16[1,64,1024]{2,1,0:T(8,128)(2,1)S(1)} %maximum_bitcast_fusion.1), channel_id=1, source_target_pairs={{0,8},{4,12},{8,0},{12,4},{16,24},{20,28},{24,16},{28,20},{1,9},{5... | collective-permute-start | bytes 393224 | tf_op jit(solution)/shard_map/A0c1m0/ppermute | solution.py:19
  45.5 4.2 %collective-permute-start.20 = (bf16[64,256]{1,0:T(8,128)(2,1)S(1)}, bf16[64,256]{1,0:T(8,128)(2,1)S(1)}, u32[]{:S(2)}, u32[]{:S(2)}) collective-permute-start(bf16[64,256]{1,0:T(8,128)(2,1)S(1)} %get-tuple-element.129), channel_id=1, source_target_pairs={{0,1},{1,0},{2,3},{3,2},{4,5},{5,4},{6,7},{7,6},{8,9},{9,8},{10,11... | collective-permute-start | bytes 98312 | tf_op jit(solution)/shard_map/B2m1/ppermute | solution.py:19
  49.7 6.5 %collective-permute-start.18 = (bf16[2,64,1024]{2,1,0:T(8,128)(2,1)S(1)}, bf16[2,64,1024]{2,1,0:T(8,128)(2,1)S(1)}, u32[]{:S(2)}, u32[]{:S(2)}) collective-permute-start(bf16[2,64,1024]{2,1,0:T(8,128)(2,1)S(1)} %pad_maximum_fusion.4), channel_id=1, source_target_pairs={{0,8},{4,12},{8,0},{12,4},{16,24},{20,28},{24,16},{28,20},{1,9},{5... | collective-permute-start | bytes 786440 | tf_op jit(solution)/shard_map/A1c0m0/ppermute | solution.py:19
  50.5 8.0 %collective-permute-start.25 = (bf16[1,64,1024]{2,1,0:T(8,128)(2,1)S(1)}, bf16[1,64,1024]{2,1,0:T(8,128)(2,1)S(1)}, u32[]{:S(2)}, u32[]{:S(2)}) collective-permute-start(bf16[1,64,1024]{2,1,0:T(8,128)(2,1)S(1)} %maximum_bitcast_fusion.2), channel_id=1, source_target_pairs={{0,4},{4,0},{8,12},{12,8},{16,20},{20,16},{24,28},{28,24},{1,5},{5... | collective-permute-start | bytes 393224 | tf_op jit(solution)/shard_map/A0c2m0/ppermute | solution.py:19
  52.1 5.7 %collective-permute-start.26 = (bf16[64,256]{1,0:T(8,128)(2,1)S(1)}, bf16[64,256]{1,0:T(8,128)(2,1)S(1)}, u32[]{:S(2)}, u32[]{:S(2)}) collective-permute-start(bf16[64,256]{1,0:T(8,128)(2,1)S(1)} %get-tuple-element.121), channel_id=1, source_target_pairs={{0,1},{1,0},{2,3},{3,2},{4,5},{5,4},{6,7},{7,6},{8,9},{9,8},{10,11... | collective-permute-start | bytes 98312 | tf_op jit(solution)/shard_map/B3m1/ppermute | solution.py:19
  52.2 5.6 %collective-permute-start.27 = (bf16[64,256]{1,0:T(8,128)(2,1)S(1)}, bf16[64,256]{1,0:T(8,128)(2,1)S(1)}, u32[]{:S(2)}, u32[]{:S(2)}) collective-permute-start(bf16[64,256]{1,0:T(8,128)(2,1)S(1)} %get-tuple-element.120), channel_id=1, source_target_pairs={{0,2},{1,3},{2,0},{3,1},{4,6},{5,7},{6,4},{7,5},{8,10},{9,11},{10,... | collective-permute-start | bytes 98312 | tf_op jit(solution)/shard_map/B3m2/ppermute | solution.py:19
  53.2 4.6 %collective-permute-start.28 = (bf16[64,256]{1,0:T(8,128)(2,1)S(1)}, bf16[64,256]{1,0:T(8,128)(2,1)S(1)}, u32[]{:S(2)}, u32[]{:S(2)}) collective-permute-start(bf16[64,256]{1,0:T(8,128)(2,1)S(1)} %get-tuple-element.119), channel_id=1, source_target_pairs={{0,3},{1,2},{2,1},{3,0},{4,7},{5,6},{6,5},{7,4},{8,11},{9,10},{10,... | collective-permute-start | bytes 98312 | tf_op jit(solution)/shard_map/B3m3/ppermute | solution.py:19
  56.2 6.6 %collective-permute-start.24 = (bf16[2,64,1024]{2,1,0:T(8,128)(2,1)S(1)}, bf16[2,64,1024]{2,1,0:T(8,128)(2,1)S(1)}, u32[]{:S(2)}, u32[]{:S(2)}) collective-permute-start(bf16[2,64,1024]{2,1,0:T(8,128)(2,1)S(1)} %pad_maximum_fusion.5), channel_id=1, source_target_pairs={{0,4},{4,0},{8,12},{12,8},{16,20},{20,16},{24,28},{28,24},{1,5},{5... | collective-permute-start | bytes 786440 | tf_op jit(solution)/shard_map/A1c1m0/ppermute | solution.py:19
  57.9 6.4 %collective-permute-start.30 = (bf16[1,64,1024]{2,1,0:T(8,128)(2,1)S(1)}, bf16[1,64,1024]{2,1,0:T(8,128)(2,1)S(1)}, u32[]{:S(2)}, u32[]{:S(2)}) collective-permute-start(bf16[1,64,1024]{2,1,0:T(8,128)(2,1)S(1)} %maximum_bitcast_fusion.3), channel_id=1, source_target_pairs={{0,8},{4,12},{8,0},{12,4},{16,24},{20,28},{24,16},{28,20},{1,9},{5... | collective-permute-start | bytes 393224 | tf_op jit(solution)/shard_map/A0c3m0/ppermute | solution.py:19
  58.7 9.6 %collective-permute-start.29 = (bf16[2,64,1024]{2,1,0:T(8,128)(2,1)S(1)}, bf16[2,64,1024]{2,1,0:T(8,128)(2,1)S(1)}, u32[]{:S(2)}, u32[]{:S(2)}) collective-permute-start(bf16[2,64,1024]{2,1,0:T(8,128)(2,1)S(1)} %pad_maximum_fusion.6), channel_id=1, source_target_pairs={{0,8},{4,12},{8,0},{12,4},{16,24},{20,28},{24,16},{28,20},{1,9},{5... | collective-permute-start | bytes 786440 | tf_op jit(solution)/shard_map/A1c2m0/ppermute | solution.py:19
  64.4 6.4 %collective-permute-start.31 = (bf16[2,64,1024]{2,1,0:T(8,128)(2,1)S(1)}, bf16[2,64,1024]{2,1,0:T(8,128)(2,1)S(1)}, u32[]{:S(2)}, u32[]{:S(2)}) collective-permute-start(bf16[2,64,1024]{2,1,0:T(8,128)(2,1)S(1)} %pad_maximum_fusion.7), channel_id=1, source_target_pairs={{0,4},{4,0},{8,12},{12,8},{16,20},{20,16},{24,28},{28,24},{1,5},{5... | collective-permute-start | bytes 786440 | tf_op jit(solution)/shard_map/A1c3m0/ppermute | solution.py:19
  74.5 4.3 %collective-permute-start.33 = (bf16[128,256]{1,0:T(8,128)(2,1)S(1)}, bf16[128,256]{1,0:T(8,128)(2,1)S(1)}, u32[]{:S(2)}, u32[]{:S(2)}) collective-permute-start(bf16[128,256]{1,0:T(8,128)(2,1)S(1)} %get-tuple-element.79), channel_id=1, source_target_pairs={{0,2},{1,3},{2,0},{3,1},{4,6},{5,7},{6,4},{7,5},{8,10},{9,11},{10,... | collective-permute-start | bytes 196616 | tf_op jit(solution)/shard_map/U0m2/ppermute | solution.py:19
  76.1 4.2 %collective-permute-start.34 = (bf16[128,256]{1,0:T(8,128)(2,1)S(1)}, bf16[128,256]{1,0:T(8,128)(2,1)S(1)}, u32[]{:S(2)}, u32[]{:S(2)}) collective-permute-start(bf16[128,256]{1,0:T(8,128)(2,1)S(1)} %get-tuple-element.80), channel_id=1, source_target_pairs={{0,3},{1,2},{2,1},{3,0},{4,7},{5,6},{6,5},{7,4},{8,11},{9,10},{10,... | collective-permute-start | bytes 196616 | tf_op jit(solution)/shard_map/U0m3/ppermute | solution.py:19
  (7 other events, 22.7 us)

commit v3 on v2

--- a/solution.py
+++ b/solution.py
@@ -8,9 +8,15 @@
 from jax.sharding import PartitionSpec as P
 
 stat_decay = 0.9
-chunk_parts = (1,1,1,1)
+chunk_parts = (1, 1, 1, 1)
 sum_ways = (1,)
-gather_ways = (1, -1,)
+gather_ways = (1, -1, 1, -1,)
+groups = ((0,), (1,), (2,), (3,))
+steps = (
+    "s00", "s10", "s01", "s20", "s11", "s30", "s21", "s02", "g00", "s31",
+    "s12", "g01", "g10", "s22", "g20", "g11", "s32", "g30", "g02", "g21",
+    "g31", "g12", "g22", "g03", "g32", "g13", "g23", "g33",
+)
 vmem_bytes = 24 * 2**20
 
 
@@ -39,14 +45,27 @@
     return list(zip(edges[:-1], edges[1:]))
 
 
-def wave(count, stages):
-    return [
-        (k, s)
-        for turn in range(count * 1 + stages)
-        for k in reversed(range(count))
-        for s in range(stages)
-        if k * 1 + s == turn
-    ]
+def steps_of(bits):
+    if bits == 2:
+        return [(name[0], int(name[1]), int(name[2])) for name in steps]
+    stage_of = lambda given, k: (bits if given[k % len(given)] else 1) + 1
+    sums = [("s", k, s) for k in range(len(chunk_parts)) for s in range(stage_of(sum_ways, k))]
+    sums.sort(key=lambda step: (step[1] + step[2], -step[1]))
+    gathers = [("g", g, s) for g in range(len(groups)) for s in range(stage_of(gather_ways, g) + 1)]
+    return sums + sorted(gathers, key=lambda step: (step[1] + step[2], -step[1]))
+
+
+def hold(values, earlier):
+    anywhere = pl.BlockSpec(memory_space=pl.ANY)
+    return pl.pallas_call(
+        lambda *refs: None,
+        in_specs=[anywhere, anywhere],
+        out_specs=anywhere,
+        out_shape=jax.ShapeDtypeStruct(values.shape, values.dtype),
+        input_output_aliases={0: 0},
+        compiler_params=pltpu.CompilerParams(vmem_limit_bytes=2**20),
+        cost_estimate=pl.CostEstimate(flops=1000, bytes_accessed=1000, transcendentals=0),
+    )(values, earlier)
 
 
 def update_kernel(count, blk_ref, *refs):
@@ -132,7 +151,6 @@
     strip_rows = left_old.shape[1]
     dp_index = lax.axis_index("dp")
     blk_index = lax.axis_index("blk")
-    place = [(dp_index >> j) & 1 for j in range(bits)]
     cols = grads.shape[3]
     spans = chunks_of(block_size)
     state = {}
@@ -141,92 +159,124 @@
     def after(values):
         if last[0] is None:
             return values
-        return lax.optimization_barrier((values, last[0]))[0]
-
-    def dim_of(j, taken):
-        return 1 + len([i for i in range(bits) if i > j and i not in taken])
-
-    def send(k, s, values):
-        with jax.named_scope(f"R{s}c{k}m0"):
-            return swap(values, "dp", 1 << rs_order(k)[s])
-
-    def rs_order(k):
-        return list(range(bits))[:: sum_ways[k % len(sum_ways)]]
-
-    def ag_order(k):
-        return list(range(bits))[:: gather_ways[k % len(gather_ways)]]
-
-    def part_of(k, j, index):
+        leaves, tree = jax.tree.flatten(values)
+        leaves[0] = hold(leaves[0], jax.tree.leaves(last[0])[0])
+        return jax.tree.unflatten(tree, leaves)
+
+    def ways(given, k):
+        way = given[k % len(given)]
+        return [[j] for j in range(bits)][::way] if way else [list(range(bits))]
+
+    def mask_of(group, which):
+        return sum(1 << j for i, j in enumerate(group) if which >> i & 1)
+
+    def pick_place(values, places, group, mask):
+        rest = [p for p in places if not any(p >> j & 1 for j in group)]
+        mine = sum(((dp_index ^ mask) >> j & 1) << i for i, j in enumerate(group))
+        if len(rest) > 1 and len(group) == 1:
+            inner = 1 << len([j for j in range(bits) if j < group[0] and any(p >> j & 1 for p in places)])
+            shape = values.shape
+            split = values.reshape(shape[0], len(places) // (2 * inner), 2, inner, *shape[2:])
+            return pick(split, mine, 2).reshape(shape[0], len(rest), *shape[2:]), rest
+        return lax.dynamic_slice_in_dim(values, mine, 1, 1), rest
+
+    def chunk(k):
         start, stop = spans[k]
-        high, depth = 2 ** (bits - 1 - j), (stop - start) // near
-        low = 2**j * depth
-        rows = grads[0, :, start:stop].reshape(owners, high, 2, low, cols)
-        rows = lax.dynamic_slice_in_dim(rows, index, 1, 2)
-        return rows.reshape(owners, *([2] * (bits - 1)), depth, cols)
+        return grads[0, :, start:stop].reshape(owners, near, (stop - start) // near, cols)
+
+    def send_sum(k, values, places, group):
+        sent, parts = [], []
+        for which in range(1, 1 << len(group)):
+            mask = mask_of(group, which)
+            with jax.named_scope(f"R{group[0]}c{k}m{mask}"):
+                part = pick_place(values, places, group, mask)[0].astype(jnp.bfloat16)
+                sent.append(swap(part, "dp", mask))
+                parts.append(part)
+        return sent, parts
+
+    def send_gather(k, strip, group):
+        sent = []
+        for which in range(1, 1 << len(group)):
+            mask = mask_of(group, which)
+            with jax.named_scope(f"A{group[0]}c{k}m{mask}"):
+                sent.append(swap(strip, "dp", mask))
+        return sent
 
     def first(k):
-        j = rs_order(k)[0]
-        state[k] = send(k, 0, part_of(k, j, 1 - place[j]))
-
-    def step(k, s):
-        order = rs_order(k)
-        if s < bits:
-            if s == 0:
-                own, received = part_of(k, order[0], place[order[0]]), after(state[k])
+        places = list(range(near))
+        group = ways(sum_ways, k)[0]
+        state[k] = (chunk(k), places, send_sum(k, chunk(k), places, group)[0])
+
+    def sum_step(k, s):
+        sums = ways(sum_ways, k)
+        if s < len(sums):
+            values, places, received = state[k]
+            received = after(received)
+            own, places = pick_place(values, places, sums[s], 0)
+            total = own.astype(jnp.float32)
+            for piece in received:
+                total = total + piece.astype(jnp.float32)
+            if s + 1 < len(sums):
+                sent, last[0] = send_sum(k, total, places, sums[s + 1])
+                state[k] = (total, places, sent)
             else:
-                own, received = state[k]
-                received = after(received)
-                own = pick(own, place[order[s]], dim_of(order[s], order[:s]))
-            total = own.astype(jnp.float32) + received.astype(jnp.float32)
-            if s + 1 < bits:
-                j = order[s + 1]
-                sent = pick(total, 1 - place[j], dim_of(j, order[: s + 1])).astype(jnp.bfloat16)
-                state[k] = (total, send(k, s + 1, sent))
-            else:
-                sent = total.astype(jnp.bfloat16)
+                total = total[:, 0]
+                last[0] = total.astype(jnp.bfloat16)
                 with jax.named_scope(f"Z{k}m0"):
-                    state[k] = (total, swap(sent, "dp", near))
-            last[0] = sent
-        elif s == bits:
+                    state[k] = (total, swap(last[0], "dp", near))
+        else:
             total, far = state[k]
             far = after(far)
-            owned = (total + far.astype(jnp.float32)).astype(jnp.bfloat16)
-            state[k] = [pick(owned, blk_index, 0)]
+            last[0] = (total + far.astype(jnp.float32)).astype(jnp.bfloat16)
+            state[k] = last[0]
+
+    def gather_step(g, s):
+        gathers = ways(gather_ways, g)
+        if s == 0:
+            owned = [state[k] for k in groups[g]]
+            owned = jnp.concatenate(owned, axis=1) if len(owned) > 1 else owned[0]
+            if len(groups[g]) > 1:
+                owned = after(owned)
+            pieces = [pick(owned, blk_index, 0)]
             for m in range(1, owners):
-                with jax.named_scope(f"B{k}m{m}"):
-                    state[k].append(swap(pick(owned, blk_index ^ m, 0), "blk", m))
-            last[0] = owned
+                with jax.named_scope(f"B{g}m{m}"):
+                    pieces.append(swap(pick(owned, blk_index ^ m, 0), "blk", m))
+            state["g", g] = pieces
+            if len(groups[g]) > 1:
+                last[0] = owned
+            return
+        if s == 1:
+            pieces = after(state["g", g])
+            strip = jnp.concatenate(ordered(pieces, blk_index), axis=1)[None]
         else:
-            g = s - bits - 1
-            if g == 0:
-                pieces = after(state[k])
-                strip = jnp.concatenate(ordered(pieces, blk_index), axis=1)[None]
-            else:
-                strip, other = state[k]
-                other = after(other)
-                j = ag_order(k)[g - 1]
-                strip = jnp.concatenate(ordered([strip, other], place[j]), axis=0)
-            last[0] = strip
-            if g < bits:
-                with jax.named_scope(f"A{g}c{k}m0"):
-                    state[k] = (strip, swap(strip, "dp", 1 << ag_order(k)[g]))
-            else:
-                state[k] = strip
-
-    order = [] or wave(len(spans), 2 * bits + 2)
+            strip, others = state["g", g]
+            others = after(others)
+            group = gathers[s - 2]
+            mine = sum((dp_index >> j & 1) << i for i, j in enumerate(group))
+            strip = jnp.concatenate(ordered([strip] + others, mine), axis=0)
+        last[0] = strip
+        if s - 1 < len(gathers):
+            state["g", g] = (strip, send_gather(g, strip, gathers[s - 1]))
+        else:
+            state["g", g] = strip
+
     for k in range(len(spans)):
         first(k)
-    for k, s in order:
-        step(k, s)
+    for kind, index, stage in steps_of(bits):
+        (sum_step if kind == "s" else gather_step)(index, stage)
     strips = []
-    for k in range(len(spans)):
+    for g in range(len(groups)):
         places = [0]
-        for j in ag_order(k):
-            places = places + [p + (1 << j) for p in places]
-        strip = state[k]
+        for group in ways(gather_ways, g):
+            places = [p + mask_of(group, w) for w in range(1 << len(group)) for p in places]
+        strip = state["g", g]
         if places != list(range(near)):
             strip = jnp.concatenate([strip[places.index(p)][None] for p in range(near)], axis=0)
-        strips.append(strip.reshape(-1, block_size))
+        start = 0
+        for k in groups[g]:
+            depth = (spans[k][1] - spans[k][0]) // near
+            strips.append(strip[:, start : start + depth].reshape(-1, block_size))
+            start += depth
 
     aligned = cols % 128 == 0 and strip_rows % 128 == 0
     if aligned:

time: 81.3 us -> 77.5 us (0.953)
  waiting for transfers between devices: 28 us -> 24.2 us
  starting transfers between devices: 39.5 us -> 43 us
  other arithmetic: 5.07 us -> 3.22 us
  local copies, waits for them, and re-layouts: 3.93 us -> 2.35 us
    ppermute x35, waiting for transfers between devices: 28 us -> 24.2 us  [swap(): return lax.ppermute(values, axis, [(i, i ^ mask) for i in range(size)])]
    ppermute x35, starting transfers between devices: 39.5 us -> 43 us  [swap(): return lax.ppermute(values, axis, [(i, i ^ mask) for i in range(size)])]
    add x4, other arithmetic: 3.08 us -> 1.18 us  [sum_step(): total = total + piece.astype(jnp.float32)]
    unnamed x8, local copies, waits for them, and re-layouts: 1.95 us -> 0.18 us
  transfers between devices with their start and end apart: 35 -> 35, of which waited for: 14 -> 16; matrix products, arithmetic and copies ran while one was open for 5% -> 4% of each run, Pallas kernels for 2% -> 3%
where the time goes in v3:
time: 77.5 us; the launch traced here: 77.3 us
  starting transfers between devices  43 us (55%)
  waiting for transfers between devices  24.2 us (31%)
  Pallas kernels  3.41 us (4%)
  other arithmetic  3.22 us (4%)
  local copies, waits for them, and re-layouts  2.35 us (3%)
  between operations  1.2 us (2%)
    ppermute x35, starting transfers between devices, swap(): return lax.ppermute(values, axis, [(i, i ^ mask) for i in range(size)])  43 us
    ppermute x35, waiting for transfers between devices, swap(): return lax.ppermute(values, axis, [(i, i ^ mask) for i in range(size)])  24.2 us
    pallas_call x1, Pallas kernels, make_stats(): pl.pallas_call(functools.partial(stat_kernel, len(strips)), in_specs=[pl....  2.01 us
    slice x1, local copies, waits for them, and re-layouts, chunk(): grads[0, :, start:stop].reshape(owners, near, (stop - start) // near, cols)  1.66 us
  transfers between devices with their start and end apart: 35, of which 16 were waited for; matrix products, arithmetic and copies ran while one was open for 4% of the time, Pallas kernels for 3%

profile of v3, /device:TPU:0, one launch (start us, length us, event | category | flops | bytes accessed | tf_op | source)
XLA Modules:
  0.0 77.3 jit_solution(12241344422146481067)
XLA Ops:
  0.6 1.7 %fusion.4 = (bf16[1,4,256,256]{3,2,1,0:T(8,128)(2,1)S(1)}, bf16[1,4,256,256]{3,2,1,0:T(8,128)(2,1)S(1)}, bf16[1,4,256,256]{3,2,1,0:T(8,128)(2,1)S(1)}, bf16[1,4,256,256]{3,2,1,0:T(8,128)(2,1)S(1)}) fusion(bf16[1,4,1024,256]{3,2,1,0:T(8,128)(2,1)} %param.5), kind=kLoop, calls=%fused_computation.104 | loop fusion | bytes 4194304 | tf_op jit(solution)/shard_map/slice | solution.py:185
  2.4 3.0 %collective-permute-start = (bf16[4,2,64,256]{3,2,0,1:T(8,128)(2,1)S(1)}, bf16[4,2,64,256]{3,2,0,1:T(8,128)(2,1)}, u32[]{:S(2)}, u32[]{:S(2)}) collective-permute-start(bf16[4,2,64,256]{3,2,0,1:T(8,128)(2,1)S(1)} %bitcast.163), channel_id=1, source_target_pairs={{0,4},{4,0},{8,12},{12,8},{16,20},{20,16},{24,28},{28,24},{1,5},{5... | collective-permute-start | bytes 786440 | tf_op jit(solution)/shard_map/R0c0m1/ppermute | solution.py:25
  5.6 2.1 %collective-permute-start.4 = (bf16[4,2,64,256]{3,2,1,0:T(8,128)(2,1)S(1)}, bf16[4,2,64,256]{3,2,1,0:T(8,128)(2,1)S(1)}, u32[]{:S(2)}, u32[]{:S(2)}) collective-permute-start(bf16[4,2,64,256]{3,2,1,0:T(8,128)(2,1)S(1)} %get-tuple-element.29), channel_id=1, source_target_pairs={{0,4},{4,0},{8,12},{12,8},{16,20},{20,16},{24,28},{28,24},{1,5},{5... | collective-permute-start | bytes 786440 | tf_op jit(solution)/shard_map/R0c2m1/ppermute | solution.py:25
  7.9 4.7 %collective-permute-done = bf16[4,2,64,256]{3,2,0,1:T(8,128)(2,1)} collective-permute-done((bf16[4,2,64,256]{3,2,0,1:T(8,128)(2,1)S(1)}, bf16[4,2,64,256]{3,2,0,1:T(8,128)(2,1)}, u32[]{:S(2)}, u32[]{:S(2)}) %collective-permute-start) | collective-permute-done | bytes 262176 | tf_op jit(solution)/shard_map/R0c0m1/ppermute | solution.py:25
  12.7 1.0 %convert_add_fusion.3 = f32[4,2,64,256]{3,2,0,1:T(8,128)S(1)} fusion(bf16[4,2,64,256]{3,2,0,1:T(8,128)(2,1)} %collective-permute-done, bf16[4,2,1,1,64,256]{5,4,2,1,0,3:T(8,128)(2,1)S(1)} %get-tuple-element.33), kind=kLoop, calls=%fused_computation.8 | loop fusion | flops 393216 | bytes 1048576 | tf_op jit(solution)/shard_map/add | solution.py:218
  13.7 2.2 %collective-permute-start.1 = (bf16[4,1,64,256]{3,2,0,1:T(8,128)(2,1)S(1)}, bf16[4,1,64,256]{3,2,0,1:T(8,128)(2,1)S(1)}, u32[]{:S(2)}, u32[]{:S(2)}) collective-permute-start(bf16[4,1,64,256]{3,2,0,1:T(8,128)(2,1)S(1)} %dynamic-slice_convert_fusion.3), channel_id=1, source_target_pairs={{0,8},{4,12},{8,0},{12,4},{16,24},{20,28},{24,16},{28,20},{1,9},{5... | collective-permute-start | bytes 393224 | tf_op jit(solution)/shard_map/R1c0m2/ppermute | solution.py:25
  15.9 2.3 %collective-permute-done.2.refs_0_ = bf16[4,2,64,256]{3,2,1,0:T(8,128)(2,1)S(1)} collective-permute-done((bf16[4,2,64,256]{3,2,1,0:T(8,128)(2,1)S(1)}, bf16[4,2,64,256]{3,2,1,0:T(8,128)(2,1)S(1)}, u32[]{:S(2)}, u32[]{:S(2)}) %collective-permute-start.2) | collective-permute-done | bytes 262176 | tf_op jit(solution)/shard_map/R0c1m1/ppermute | solution.py:25
  18.3 2.2 %collective-permute-start.7 = (bf16[4,1,64,256]{3,2,0,1:T(8,128)(2,1)S(1)}, bf16[4,1,64,256]{3,2,0,1:T(8,128)(2,1)S(1)}, u32[]{:S(2)}, u32[]{:S(2)}) collective-permute-start(bf16[4,1,64,256]{3,2,0,1:T(8,128)(2,1)S(1)} %dynamic-slice_convert_fusion.2), channel_id=1, source_target_pairs={{0,8},{4,12},{8,0},{12,4},{16,24},{20,28},{24,16},{28,20},{1,9},{5... | collective-permute-start | bytes 393224 | tf_op jit(solution)/shard_map/R1c1m2/ppermute | solution.py:25
  20.5 2.7 %collective-permute-start.3 = (bf16[4,64,256]{2,1,0:T(8,128)(2,1)S(1)}, bf16[4,64,256]{2,1,0:T(8,128)(2,1)S(1)}, u32[]{:S(2)}, u32[]{:S(2)}) collective-permute-start(bf16[4,64,256]{2,1,0:T(8,128)(2,1)S(1)} %bitcast_convert_fusion.3.refs_1_), channel_id=1, source_target_pairs={{0,16},{4,20},{8,24},{12,28},{16,0},{20,4},{24,8},{28,12},{1,17},{... | collective-permute-start | bytes 393224 | tf_op jit(solution)/shard_map/Z0m0/ppermute | solution.py:25
  23.9 2.2 %collective-permute-start.5 = (bf16[4,1,64,256]{3,2,0,1:T(8,128)(2,1)S(1)}, bf16[4,1,64,256]{3,2,0,1:T(8,128)(2,1)S(1)}, u32[]{:S(2)}, u32[]{:S(2)}) collective-permute-start(bf16[4,1,64,256]{3,2,0,1:T(8,128)(2,1)S(1)} %dynamic-slice_convert_fusion.1), channel_id=1, source_target_pairs={{0,8},{4,12},{8,0},{12,4},{16,24},{20,28},{24,16},{28,20},{1,9},{5... | collective-permute-start | bytes 393224 | tf_op jit(solution)/shard_map/R1c2m2/ppermute | solution.py:25
  26.1 2.7 %collective-permute-start.8 = (bf16[4,64,256]{2,1,0:T(8,128)(2,1)S(1)}, bf16[4,64,256]{2,1,0:T(8,128)(2,1)S(1)}, u32[]{:S(2)}, u32[]{:S(2)}) collective-permute-start(bf16[4,64,256]{2,1,0:T(8,128)(2,1)S(1)} %bitcast_convert_fusion.2.refs_1_), channel_id=1, source_target_pairs={{0,16},{4,20},{8,24},{12,28},{16,0},{20,4},{24,8},{28,12},{1,17},{... | collective-permute-start | bytes 393224 | tf_op jit(solution)/shard_map/Z1m0/ppermute | solution.py:25
  28.9 1.6 %collective-permute-start.9 = (bf16[4,1,64,256]{3,2,0,1:T(8,128)(2,1)S(1)}, bf16[4,1,64,256]{3,2,0,1:T(8,128)(2,1)S(1)}, u32[]{:S(2)}, u32[]{:S(2)}) collective-permute-start(bf16[4,1,64,256]{3,2,0,1:T(8,128)(2,1)S(1)} %dynamic-slice_convert_fusion), channel_id=1, source_target_pairs={{0,8},{4,12},{8,0},{12,4},{16,24},{20,28},{24,16},{28,20},{1,9},{5... | collective-permute-start | bytes 393224 | tf_op jit(solution)/shard_map/R1c3m2/ppermute | solution.py:25
  30.6 2.7 %collective-permute-start.15 = (bf16[4,64,256]{2,1,0:T(8,128)(2,1)S(1)}, bf16[4,64,256]{2,1,0:T(8,128)(2,1)S(1)}, u32[]{:S(2)}, u32[]{:S(2)}) collective-permute-start(bf16[4,64,256]{2,1,0:T(8,128)(2,1)S(1)} %bitcast_convert_fusion.1.refs_1_), channel_id=1, source_target_pairs={{0,16},{4,20},{8,24},{12,28},{16,0},{20,4},{24,8},{28,12},{1,17},{... | collective-permute-start | bytes 393224 | tf_op jit(solution)/shard_map/Z2m0/ppermute | solution.py:25
  33.4 1.6 %collective-permute-start.11 = (bf16[64,256]{1,0:T(8,128)(2,1)S(1)}, bf16[64,256]{1,0:T(8,128)(2,1)S(1)}, u32[]{:S(2)}, u32[]{:S(2)}) collective-permute-start(bf16[64,256]{1,0:T(8,128)(2,1)S(1)} %get-tuple-element.83), channel_id=1, source_target_pairs={{0,2},{1,3},{2,0},{3,1},{4,6},{5,7},{6,4},{7,5},{8,10},{9,11},{10,... | collective-permute-start | bytes 98312 | tf_op jit(solution)/shard_map/B0m2/ppermute | solution.py:25
  34.9 2.1 %collective-permute-done.9 = bf16[4,1,64,256]{3,2,0,1:T(8,128)(2,1)S(1)} collective-permute-done((bf16[4,1,64,256]{3,2,0,1:T(8,128)(2,1)S(1)}, bf16[4,1,64,256]{3,2,0,1:T(8,128)(2,1)S(1)}, u32[]{:S(2)}, u32[]{:S(2)}) %collective-permute-start.9) | collective-permute-done | bytes 131104 | tf_op jit(solution)/shard_map/R1c3m2/ppermute | solution.py:25
  38.1 1.6 %collective-permute-start.17 = (bf16[64,256]{1,0:T(8,128)(2,1)S(1)}, bf16[64,256]{1,0:T(8,128)(2,1)S(1)}, u32[]{:S(2)}, u32[]{:S(2)}) collective-permute-start(bf16[64,256]{1,0:T(8,128)(2,1)S(1)} %get-tuple-element.75), channel_id=1, source_target_pairs={{0,2},{1,3},{2,0},{3,1},{4,6},{5,7},{6,4},{7,5},{8,10},{9,11},{10,... | collective-permute-start | bytes 98312 | tf_op jit(solution)/shard_map/B1m2/ppermute | solution.py:25
  40.4 1.6 %collective-permute-start.13 = (bf16[1,64,1024]{2,1,0:T(8,128)(2,1)S(1)}, bf16[1,64,1024]{2,1,0:T(8,128)(2,1)S(1)}, u32[]{:S(2)}, u32[]{:S(2)}) collective-permute-start(bf16[1,64,1024]{2,1,0:T(8,128)(2,1)S(1)} %maximum_bitcast_fusion.refs_1_), channel_id=1, source_target_pairs={{0,4},{4,0},{8,12},{12,8},{16,20},{20,16},{24,28},{28,24},{1,5},{5... | collective-permute-start | bytes 393224 | tf_op jit(solution)/shard_map/A0c0m1/ppermute | solution.py:25
  43.1 2.5 %collective-permute-start.24 = (bf16[1,64,1024]{2,1,0:T(8,128)(2,1)S(1)}, bf16[1,64,1024]{2,1,0:T(8,128)(2,1)S(1)}, u32[]{:S(2)}, u32[]{:S(2)}) collective-permute-start(bf16[1,64,1024]{2,1,0:T(8,128)(2,1)S(1)} %maximum_bitcast_fusion.1.refs_1_), channel_id=1, source_target_pairs={{0,8},{4,12},{8,0},{12,4},{16,24},{20,28},{24,16},{28,20},{1,9},{5... | collective-permute-start | bytes 393224 | tf_op jit(solution)/shard_map/A1c1m2/ppermute | solution.py:25
  45.6 1.0 %collective-permute-start.21 = (bf16[64,256]{1,0:T(8,128)(2,1)S(1)}, bf16[64,256]{1,0:T(8,128)(2,1)S(1)}, u32[]{:S(2)}, u32[]{:S(2)}) collective-permute-start(bf16[64,256]{1,0:T(8,128)(2,1)S(1)} %get-tuple-element.67), channel_id=1, source_target_pairs={{0,2},{1,3},{2,0},{3,1},{4,6},{5,7},{6,4},{7,5},{8,10},{9,11},{10,... | collective-permute-start | bytes 98312 | tf_op jit(solution)/shard_map/B2m2/ppermute | solution.py:25
  47.8 1.0 %collective-permute-start.26 = (bf16[64,256]{1,0:T(8,128)(2,1)S(1)}, bf16[64,256]{1,0:T(8,128)(2,1)S(1)}, u32[]{:S(2)}, u32[]{:S(2)}) collective-permute-start(bf16[64,256]{1,0:T(8,128)(2,1)S(1)} %get-tuple-element.59), channel_id=1, source_target_pairs={{0,2},{1,3},{2,0},{3,1},{4,6},{5,7},{6,4},{7,5},{8,10},{9,11},{10,... | collective-permute-start | bytes 98312 | tf_op jit(solution)/shard_map/B3m2/ppermute | solution.py:25
  51.8 1.5 %collective-permute-start.23 = (bf16[1,64,1024]{2,1,0:T(8,128)(2,1)S(1)}, bf16[1,64,1024]{2,1,0:T(8,128)(2,1)S(1)}, u32[]{:S(2)}, u32[]{:S(2)}) collective-permute-start(bf16[1,64,1024]{2,1,0:T(8,128)(2,1)S(1)} %maximum_bitcast_fusion.2.refs_1_), channel_id=1, source_target_pairs={{0,4},{4,0},{8,12},{12,8},{16,20},{20,16},{24,28},{28,24},{1,5},{5... | collective-permute-start | bytes 393224 | tf_op jit(solution)/shard_map/A0c2m1/ppermute | solution.py:25
  53.4 1.0 %collective-permute-start.29 = (bf16[1,64,1024]{2,1,0:T(8,128)(2,1)S(1)}, bf16[1,64,1024]{2,1,0:T(8,128)(2,1)S(1)}, u32[]{:S(2)}, u32[]{:S(2)}) collective-permute-start(bf16[1,64,1024]{2,1,0:T(8,128)(2,1)S(1)} %maximum_bitcast_fusion.3.refs_1_), channel_id=1, source_target_pairs={{0,8},{4,12},{8,0},{12,4},{16,24},{20,28},{24,16},{28,20},{1,9},{5... | collective-permute-start | bytes 393224 | tf_op jit(solution)/shard_map/A1c3m2/ppermute | solution.py:25
  55.2 1.9 %collective-permute-done.23.refs_0_ = bf16[1,64,1024]{2,1,0:T(8,128)(2,1)S(1)} collective-permute-done((bf16[1,64,1024]{2,1,0:T(8,128)(2,1)S(1)}, bf16[1,64,1024]{2,1,0:T(8,128)(2,1)S(1)}, u32[]{:S(2)}, u32[]{:S(2)}) %collective-permute-start.23) | collective-permute-done | bytes 131104 | tf_op jit(solution)/shard_map/A0c2m1/ppermute | solution.py:25
  57.3 2.1 %collective-permute-start.30 = (bf16[2,64,1024]{2,1,0:T(8,128)(2,1)S(1)}, bf16[2,64,1024]{2,1,0:T(8,128)(2,1)S(1)}, u32[]{:S(2)}, u32[]{:S(2)}) collective-permute-start(bf16[2,64,1024]{2,1,0:T(8,128)(2,1)S(1)} %pad_maximum_fusion.7.refs_1_), channel_id=1, source_target_pairs={{0,8},{4,12},{8,0},{12,4},{16,24},{20,28},{24,16},{28,20},{1,9},{5... | collective-permute-start | bytes 786440 | tf_op jit(solution)/shard_map/A1c2m2/ppermute | solution.py:25
  59.9 2.7 %collective-permute-done.29.refs_0_ = bf16[1,64,1024]{2,1,0:T(8,128)(2,1)S(1)} collective-permute-done((bf16[1,64,1024]{2,1,0:T(8,128)(2,1)S(1)}, bf16[1,64,1024]{2,1,0:T(8,128)(2,1)S(1)}, u32[]{:S(2)}, u32[]{:S(2)}) %collective-permute-start.29) | collective-permute-done | bytes 131104 | tf_op jit(solution)/shard_map/A1c3m2/ppermute | solution.py:25
  62.7 1.5 %collective-permute-start.31 = (bf16[2,64,1024]{2,1,0:T(8,128)(2,1)S(1)}, bf16[2,64,1024]{2,1,0:T(8,128)(2,1)S(1)}, u32[]{:S(2)}, u32[]{:S(2)}) collective-permute-start(bf16[2,64,1024]{2,1,0:T(8,128)(2,1)S(1)} %pad_maximum_fusion.8.refs_1_), channel_id=1, source_target_pairs={{0,4},{4,0},{8,12},{12,8},{16,20},{20,16},{24,28},{28,24},{1,5},{5... | collective-permute-start | bytes 786440 | tf_op jit(solution)/shard_map/A0c3m1/ppermute | solution.py:25
  64.5 2.9 %collective-permute-done.30.refs_0_ = bf16[2,64,1024]{2,1,0:T(8,128)(2,1)S(1)} collective-permute-done((bf16[2,64,1024]{2,1,0:T(8,128)(2,1)S(1)}, bf16[2,64,1024]{2,1,0:T(8,128)(2,1)S(1)}, u32[]{:S(2)}, u32[]{:S(2)}) %collective-permute-start.30) | collective-permute-done | bytes 262176 | tf_op jit(solution)/shard_map/A1c2m2/ppermute | solution.py:25
  67.5 1.9 %collective-permute-done.31.refs_0_ = bf16[2,64,1024]{2,1,0:T(8,128)(2,1)S(1)} collective-permute-done((bf16[2,64,1024]{2,1,0:T(8,128)(2,1)S(1)}, bf16[2,64,1024]{2,1,0:T(8,128)(2,1)S(1)}, u32[]{:S(2)}, u32[]{:S(2)}) %collective-permute-start.31) | collective-permute-done | bytes 262176 | tf_op jit(solution)/shard_map/A0c3m1/ppermute | solution.py:25
  69.7 1.4 %shard_map.99 = (bf16[128,256]{1,0:T(8,128)(2,1)S(1)}, bf16[128,256]{1,0:T(8,128)(2,1)S(1)}, bf16[128,256]{1,0:T(8,128)(2,1)S(1)}, bf16[128,256]{1,0:T(8,128)(2,1)S(1)}) custom-call(s32[2]{0:T(128)S(1)} %pad_add_fusion.blk_ref, bf16[256,1024]{1,0:T(8,128)(2,1)S(1)} %bitcast.147, bf16[256,1024]{1,0:T(8,128)(2,1)S(1)} %bitcast.151, ...), custom_call_target="tpu_custom_call" | custom-call | flops 1000 | bytes 1000 | tf_op jit(solution)/shard_map/pallas_call | solution.py:93
  71.1 1.1 %collective-permute-start.33 = (bf16[128,256]{1,0:T(8,128)(2,1)S(1)}, bf16[128,256]{1,0:T(8,128)(2,1)S(1)}, u32[]{:S(2)}, u32[]{:S(2)}) collective-permute-start(bf16[128,256]{1,0:T(8,128)(2,1)S(1)} %get-tuple-element.11), channel_id=1, source_target_pairs={{0,2},{1,3},{2,0},{3,1},{4,6},{5,7},{6,4},{7,5},{8,10},{9,11},{10,... | collective-permute-start | bytes 196616 | tf_op jit(solution)/shard_map/U0m2/ppermute | solution.py:25
  72.2 1.1 %collective-permute-start.32 = (bf16[128,256]{1,0:T(8,128)(2,1)S(1)}, bf16[128,256]{1,0:T(8,128)(2,1)S(1)}, u32[]{:S(2)}, u32[]{:S(2)}) collective-permute-start(bf16[128,256]{1,0:T(8,128)(2,1)S(1)} %get-tuple-element.10), channel_id=1, source_target_pairs={{0,1},{1,0},{2,3},{3,2},{4,5},{5,4},{6,7},{7,6},{8,9},{9,8},{10,11... | collective-permute-start | bytes 196616 | tf_op jit(solution)/shard_map/U0m1/ppermute | solution.py:25
  73.3 2.0 %shard_map.100 = (f32[1,128,1024]{2,1,0:T(8,128)}, f32[1,128,1024]{2,1,0:T(8,128)}) custom-call(s32[1]{0:T(128)} %bitcast.dp_ref, bf16[256,1024]{1,0:T(8,128)(2,1)S(1)} %bitcast.148, bf16[256,1024]{1,0:T(8,128)(2,1)S(1)} %bitcast.152, bf16[256,1024]{1,0:T(8,128)(2,1)S(1)} %bitcast.150, bf16[256,1024]{1,0:T(8,128)(2,1)S(1)} %bitcast.154, ...), custom_call_target="tpu_custom_call" | custom-call | flops 1000 | bytes 1000 | tf_op jit(solution)/shard_map/pallas_call | solution.py:135
  (131 shorter events, 12.8 us)
Async XLA Ops:
  2.4 10.3 %collective-permute-start = (bf16[4,2,64,256]{3,2,0,1:T(8,128)(2,1)S(1)}, bf16[4,2,64,256]{3,2,0,1:T(8,128)(2,1)}, u32[]{:S(2)}, u32[]{:S(2)}) collective-permute-start(bf16[4,2,64,256]{3,2,0,1:T(8,128)(2,1)S(1)} %bitcast.163), channel_id=1, source_target_pairs={{0,4},{4,0},{8,12},{12,8},{16,20},{20,16},{24,28},{28,24},{1,5},{5... | collective-permute-start | bytes 786440 | tf_op jit(solution)/shard_map/R0c0m1/ppermute | solution.py:25
  5.5 12.7 %collective-permute-start.2 = (bf16[4,2,64,256]{3,2,1,0:T(8,128)(2,1)S(1)}, bf16[4,2,64,256]{3,2,1,0:T(8,128)(2,1)S(1)}, u32[]{:S(2)}, u32[]{:S(2)}) collective-permute-start(bf16[4,2,64,256]{3,2,1,0:T(8,128)(2,1)S(1)} %get-tuple-element.31), channel_id=1, source_target_pairs={{0,4},{4,0},{8,12},{12,8},{16,20},{20,16},{24,28},{28,24},{1,5},{5... | collective-permute-start | bytes 786440 | tf_op jit(solution)/shard_map/R0c1m1/ppermute | solution.py:25
  5.6 18.2 %collective-permute-start.4 = (bf16[4,2,64,256]{3,2,1,0:T(8,128)(2,1)S(1)}, bf16[4,2,64,256]{3,2,1,0:T(8,128)(2,1)S(1)}, u32[]{:S(2)}, u32[]{:S(2)}) collective-permute-start(bf16[4,2,64,256]{3,2,1,0:T(8,128)(2,1)S(1)} %get-tuple-element.29), channel_id=1, source_target_pairs={{0,4},{4,0},{8,12},{12,8},{16,20},{20,16},{24,28},{28,24},{1,5},{5... | collective-permute-start | bytes 786440 | tf_op jit(solution)/shard_map/R0c2m1/ppermute | solution.py:25
  7.7 21.1 %collective-permute-start.6 = (bf16[4,2,64,256]{3,2,1,0:T(8,128)(2,1)S(1)}, bf16[4,2,64,256]{3,2,1,0:T(8,128)(2,1)S(1)}, u32[]{:S(2)}, u32[]{:S(2)}) collective-permute-start(bf16[4,2,64,256]{3,2,1,0:T(8,128)(2,1)S(1)} %get-tuple-element.27), channel_id=1, source_target_pairs={{0,4},{4,0},{8,12},{12,8},{16,20},{20,16},{24,28},{28,24},{1,5},{5... | collective-permute-start | bytes 786440 | tf_op jit(solution)/shard_map/R0c3m1/ppermute | solution.py:25
  13.7 6.8 %collective-permute-start.1 = (bf16[4,1,64,256]{3,2,0,1:T(8,128)(2,1)S(1)}, bf16[4,1,64,256]{3,2,0,1:T(8,128)(2,1)S(1)}, u32[]{:S(2)}, u32[]{:S(2)}) collective-permute-start(bf16[4,1,64,256]{3,2,0,1:T(8,128)(2,1)S(1)} %dynamic-slice_convert_fusion.3), channel_id=1, source_target_pairs={{0,8},{4,12},{8,0},{12,4},{16,24},{20,28},{24,16},{28,20},{1,9},{5... | collective-permute-start | bytes 393224 | tf_op jit(solution)/shard_map/R1c0m2/ppermute | solution.py:25
  18.3 7.8 %collective-permute-start.7 = (bf16[4,1,64,256]{3,2,0,1:T(8,128)(2,1)S(1)}, bf16[4,1,64,256]{3,2,0,1:T(8,128)(2,1)S(1)}, u32[]{:S(2)}, u32[]{:S(2)}) collective-permute-start(bf16[4,1,64,256]{3,2,0,1:T(8,128)(2,1)S(1)} %dynamic-slice_convert_fusion.2), channel_id=1, source_target_pairs={{0,8},{4,12},{8,0},{12,4},{16,24},{20,28},{24,16},{28,20},{1,9},{5... | collective-permute-start | bytes 393224 | tf_op jit(solution)/shard_map/R1c1m2/ppermute | solution.py:25
  20.5 12.8 %collective-permute-start.3 = (bf16[4,64,256]{2,1,0:T(8,128)(2,1)S(1)}, bf16[4,64,256]{2,1,0:T(8,128)(2,1)S(1)}, u32[]{:S(2)}, u32[]{:S(2)}) collective-permute-start(bf16[4,64,256]{2,1,0:T(8,128)(2,1)S(1)} %bitcast_convert_fusion.3.refs_1_), channel_id=1, source_target_pairs={{0,16},{4,20},{8,24},{12,28},{16,0},{20,4},{24,8},{28,12},{1,17},{... | collective-permute-start | bytes 393224 | tf_op jit(solution)/shard_map/Z0m0/ppermute | solution.py:25
  23.9 6.6 %collective-permute-start.5 = (bf16[4,1,64,256]{3,2,0,1:T(8,128)(2,1)S(1)}, bf16[4,1,64,256]{3,2,0,1:T(8,128)(2,1)S(1)}, u32[]{:S(2)}, u32[]{:S(2)}) collective-permute-start(bf16[4,1,64,256]{3,2,0,1:T(8,128)(2,1)S(1)} %dynamic-slice_convert_fusion.1), channel_id=1, source_target_pairs={{0,8},{4,12},{8,0},{12,4},{16,24},{20,28},{24,16},{28,20},{1,9},{5... | collective-permute-start | bytes 393224 | tf_op jit(solution)/shard_map/R1c2m2/ppermute | solution.py:25
  26.1 11.8 %collective-permute-start.8 = (bf16[4,64,256]{2,1,0:T(8,128)(2,1)S(1)}, bf16[4,64,256]{2,1,0:T(8,128)(2,1)S(1)}, u32[]{:S(2)}, u32[]{:S(2)}) collective-permute-start(bf16[4,64,256]{2,1,0:T(8,128)(2,1)S(1)} %bitcast_convert_fusion.2.refs_1_), channel_id=1, source_target_pairs={{0,16},{4,20},{8,24},{12,28},{16,0},{20,4},{24,8},{28,12},{1,17},{... | collective-permute-start | bytes 393224 | tf_op jit(solution)/shard_map/Z1m0/ppermute | solution.py:25
  28.9 8.1 %collective-permute-start.9 = (bf16[4,1,64,256]{3,2,0,1:T(8,128)(2,1)S(1)}, bf16[4,1,64,256]{3,2,0,1:T(8,128)(2,1)S(1)}, u32[]{:S(2)}, u32[]{:S(2)}) collective-permute-start(bf16[4,1,64,256]{3,2,0,1:T(8,128)(2,1)S(1)} %dynamic-slice_convert_fusion), channel_id=1, source_target_pairs={{0,8},{4,12},{8,0},{12,4},{16,24},{20,28},{24,16},{28,20},{1,9},{5... | collective-permute-start | bytes 393224 | tf_op jit(solution)/shard_map/R1c3m2/ppermute | solution.py:25
  30.6 9.8 %collective-permute-start.15 = (bf16[4,64,256]{2,1,0:T(8,128)(2,1)S(1)}, bf16[4,64,256]{2,1,0:T(8,128)(2,1)S(1)}, u32[]{:S(2)}, u32[]{:S(2)}) collective-permute-start(bf16[4,64,256]{2,1,0:T(8,128)(2,1)S(1)} %bitcast_convert_fusion.1.refs_1_), channel_id=1, source_target_pairs={{0,16},{4,20},{8,24},{12,28},{16,0},{20,4},{24,8},{28,12},{1,17},{... | collective-permute-start | bytes 393224 | tf_op jit(solution)/shard_map/Z2m0/ppermute | solution.py:25
  33.4 4.8 %collective-permute-start.11 = (bf16[64,256]{1,0:T(8,128)(2,1)S(1)}, bf16[64,256]{1,0:T(8,128)(2,1)S(1)}, u32[]{:S(2)}, u32[]{:S(2)}) collective-permute-start(bf16[64,256]{1,0:T(8,128)(2,1)S(1)} %get-tuple-element.83), channel_id=1, source_target_pairs={{0,2},{1,3},{2,0},{3,1},{4,6},{5,7},{6,4},{7,5},{8,10},{9,11},{10,... | collective-permute-start | bytes 98312 | tf_op jit(solution)/shard_map/B0m2/ppermute | solution.py:25
  34.9 4.8 %collective-permute-start.12 = (bf16[64,256]{1,0:T(8,128)(2,1)S(1)}, bf16[64,256]{1,0:T(8,128)(2,1)S(1)}, u32[]{:S(2)}, u32[]{:S(2)}) collective-permute-start(bf16[64,256]{1,0:T(8,128)(2,1)S(1)} %get-tuple-element.84), channel_id=1, source_target_pairs={{0,3},{1,2},{2,1},{3,0},{4,7},{5,6},{6,5},{7,4},{8,11},{9,10},{10,... | collective-permute-start | bytes 98312 | tf_op jit(solution)/shard_map/B0m3/ppermute | solution.py:25
  37.1 8.5 %collective-permute-start.14 = (bf16[4,64,256]{2,1,0:T(8,128)(2,1)S(1)}, bf16[4,64,256]{2,1,0:T(8,128)(2,1)S(1)}, u32[]{:S(2)}, u32[]{:S(2)}) collective-permute-start(bf16[4,64,256]{2,1,0:T(8,128)(2,1)S(1)} %bitcast_convert_fusion.refs_1_), channel_id=1, source_target_pairs={{0,16},{4,20},{8,24},{12,28},{16,0},{20,4},{24,8},{28,12},{1,17},{... | collective-permute-start | bytes 393224 | tf_op jit(solution)/shard_map/Z3m0/ppermute | solution.py:25
  38.1 4.0 %collective-permute-start.17 = (bf16[64,256]{1,0:T(8,128)(2,1)S(1)}, bf16[64,256]{1,0:T(8,128)(2,1)S(1)}, u32[]{:S(2)}, u32[]{:S(2)}) collective-permute-start(bf16[64,256]{1,0:T(8,128)(2,1)S(1)} %get-tuple-element.75), channel_id=1, source_target_pairs={{0,2},{1,3},{2,0},{3,1},{4,6},{5,7},{6,4},{7,5},{8,10},{9,11},{10,... | collective-permute-start | bytes 98312 | tf_op jit(solution)/shard_map/B1m2/ppermute | solution.py:25
  39.7 3.3 %collective-permute-start.18 = (bf16[64,256]{1,0:T(8,128)(2,1)S(1)}, bf16[64,256]{1,0:T(8,128)(2,1)S(1)}, u32[]{:S(2)}, u32[]{:S(2)}) collective-permute-start(bf16[64,256]{1,0:T(8,128)(2,1)S(1)} %get-tuple-element.76), channel_id=1, source_target_pairs={{0,3},{1,2},{2,1},{3,0},{4,7},{5,6},{6,5},{7,4},{8,11},{9,10},{10,... | collective-permute-start | bytes 98312 | tf_op jit(solution)/shard_map/B1m3/ppermute | solution.py:25
  40.4 7.5 %collective-permute-start.13 = (bf16[1,64,1024]{2,1,0:T(8,128)(2,1)S(1)}, bf16[1,64,1024]{2,1,0:T(8,128)(2,1)S(1)}, u32[]{:S(2)}, u32[]{:S(2)}) collective-permute-start(bf16[1,64,1024]{2,1,0:T(8,128)(2,1)S(1)} %maximum_bitcast_fusion.refs_1_), channel_id=1, source_target_pairs={{0,4},{4,0},{8,12},{12,8},{16,20},{20,16},{24,28},{28,24},{1,5},{5... | collective-permute-start | bytes 393224 | tf_op jit(solution)/shard_map/A0c0m1/ppermute | solution.py:25
  43.1 11.3 %collective-permute-start.24 = (bf16[1,64,1024]{2,1,0:T(8,128)(2,1)S(1)}, bf16[1,64,1024]{2,1,0:T(8,128)(2,1)S(1)}, u32[]{:S(2)}, u32[]{:S(2)}) collective-permute-start(bf16[1,64,1024]{2,1,0:T(8,128)(2,1)S(1)} %maximum_bitcast_fusion.1.refs_1_), channel_id=1, source_target_pairs={{0,8},{4,12},{8,0},{12,4},{16,24},{20,28},{24,16},{28,20},{1,9},{5... | collective-permute-start | bytes 393224 | tf_op jit(solution)/shard_map/A1c1m2/ppermute | solution.py:25
  45.6 4.0 %collective-permute-start.21 = (bf16[64,256]{1,0:T(8,128)(2,1)S(1)}, bf16[64,256]{1,0:T(8,128)(2,1)S(1)}, u32[]{:S(2)}, u32[]{:S(2)}) collective-permute-start(bf16[64,256]{1,0:T(8,128)(2,1)S(1)} %get-tuple-element.67), channel_id=1, source_target_pairs={{0,2},{1,3},{2,0},{3,1},{4,6},{5,7},{6,4},{7,5},{8,10},{9,11},{10,... | collective-permute-start | bytes 98312 | tf_op jit(solution)/shard_map/B2m2/ppermute | solution.py:25
  46.6 3.6 %collective-permute-start.22 = (bf16[64,256]{1,0:T(8,128)(2,1)S(1)}, bf16[64,256]{1,0:T(8,128)(2,1)S(1)}, u32[]{:S(2)}, u32[]{:S(2)}) collective-permute-start(bf16[64,256]{1,0:T(8,128)(2,1)S(1)} %get-tuple-element.68), channel_id=1, source_target_pairs={{0,3},{1,2},{2,1},{3,0},{4,7},{5,6},{6,5},{7,4},{8,11},{9,10},{10,... | collective-permute-start | bytes 98312 | tf_op jit(solution)/shard_map/B2m3/ppermute | solution.py:25
  47.0 3.7 %collective-permute-start.20 = (bf16[64,256]{1,0:T(8,128)(2,1)S(1)}, bf16[64,256]{1,0:T(8,128)(2,1)S(1)}, u32[]{:S(2)}, u32[]{:S(2)}) collective-permute-start(bf16[64,256]{1,0:T(8,128)(2,1)S(1)} %get-tuple-element.69), channel_id=1, source_target_pairs={{0,1},{1,0},{2,3},{3,2},{4,5},{5,4},{6,7},{7,6},{8,9},{9,8},{10,11... | collective-permute-start | bytes 98312 | tf_op jit(solution)/shard_map/B2m1/ppermute | solution.py:25
  47.8 4.0 %collective-permute-start.26 = (bf16[64,256]{1,0:T(8,128)(2,1)S(1)}, bf16[64,256]{1,0:T(8,128)(2,1)S(1)}, u32[]{:S(2)}, u32[]{:S(2)}) collective-permute-start(bf16[64,256]{1,0:T(8,128)(2,1)S(1)} %get-tuple-element.59), channel_id=1, source_target_pairs={{0,2},{1,3},{2,0},{3,1},{4,6},{5,7},{6,4},{7,5},{8,10},{9,11},{10,... | collective-permute-start | bytes 98312 | tf_op jit(solution)/shard_map/B3m2/ppermute | solution.py:25
  49.6 3.8 %collective-permute-start.27 = (bf16[64,256]{1,0:T(8,128)(2,1)S(1)}, bf16[64,256]{1,0:T(8,128)(2,1)S(1)}, u32[]{:S(2)}, u32[]{:S(2)}) collective-permute-start(bf16[64,256]{1,0:T(8,128)(2,1)S(1)} %get-tuple-element.60), channel_id=1, source_target_pairs={{0,3},{1,2},{2,1},{3,0},{4,7},{5,6},{6,5},{7,4},{8,11},{9,10},{10,... | collective-permute-start | bytes 98312 | tf_op jit(solution)/shard_map/B3m3/ppermute | solution.py:25
  50.7 9.2 %collective-permute-start.19 = (bf16[2,64,1024]{2,1,0:T(8,128)(2,1)S(1)}, bf16[2,64,1024]{2,1,0:T(8,128)(2,1)S(1)}, u32[]{:S(2)}, u32[]{:S(2)}) collective-permute-start(bf16[2,64,1024]{2,1,0:T(8,128)(2,1)S(1)} %pad_maximum_fusion.5.refs_1_), channel_id=1, source_target_pairs={{0,8},{4,12},{8,0},{12,4},{16,24},{20,28},{24,16},{28,20},{1,9},{5... | collective-permute-start | bytes 786440 | tf_op jit(solution)/shard_map/A1c0m2/ppermute | solution.py:25
  51.8 5.3 %collective-permute-start.23 = (bf16[1,64,1024]{2,1,0:T(8,128)(2,1)S(1)}, bf16[1,64,1024]{2,1,0:T(8,128)(2,1)S(1)}, u32[]{:S(2)}, u32[]{:S(2)}) collective-permute-start(bf16[1,64,1024]{2,1,0:T(8,128)(2,1)S(1)} %maximum_bitcast_fusion.2.refs_1_), channel_id=1, source_target_pairs={{0,4},{4,0},{8,12},{12,8},{16,20},{20,16},{24,28},{28,24},{1,5},{5... | collective-permute-start | bytes 393224 | tf_op jit(solution)/shard_map/A0c2m1/ppermute | solution.py:25
  53.4 9.3 %collective-permute-start.29 = (bf16[1,64,1024]{2,1,0:T(8,128)(2,1)S(1)}, bf16[1,64,1024]{2,1,0:T(8,128)(2,1)S(1)}, u32[]{:S(2)}, u32[]{:S(2)}) collective-permute-start(bf16[1,64,1024]{2,1,0:T(8,128)(2,1)S(1)} %maximum_bitcast_fusion.3.refs_1_), channel_id=1, source_target_pairs={{0,8},{4,12},{8,0},{12,4},{16,24},{20,28},{24,16},{28,20},{1,9},{5... | collective-permute-start | bytes 393224 | tf_op jit(solution)/shard_map/A1c3m2/ppermute | solution.py:25
  54.5 9.8 %collective-permute-start.28 = (bf16[2,64,1024]{2,1,0:T(8,128)(2,1)S(1)}, bf16[2,64,1024]{2,1,0:T(8,128)(2,1)S(1)}, u32[]{:S(2)}, u32[]{:S(2)}) collective-permute-start(bf16[2,64,1024]{2,1,0:T(8,128)(2,1)S(1)} %pad_maximum_fusion.6.refs_1_), channel_id=1, source_target_pairs={{0,4},{4,0},{8,12},{12,8},{16,20},{20,16},{24,28},{28,24},{1,5},{5... | collective-permute-start | bytes 786440 | tf_op jit(solution)/shard_map/A0c1m1/ppermute | solution.py:25
  57.3 10.1 %collective-permute-start.30 = (bf16[2,64,1024]{2,1,0:T(8,128)(2,1)S(1)}, bf16[2,64,1024]{2,1,0:T(8,128)(2,1)S(1)}, u32[]{:S(2)}, u32[]{:S(2)}) collective-permute-start(bf16[2,64,1024]{2,1,0:T(8,128)(2,1)S(1)} %pad_maximum_fusion.7.refs_1_), channel_id=1, source_target_pairs={{0,8},{4,12},{8,0},{12,4},{16,24},{20,28},{24,16},{28,20},{1,9},{5... | collective-permute-start | bytes 786440 | tf_op jit(solution)/shard_map/A1c2m2/ppermute | solution.py:25
  62.7 6.6 %collective-permute-start.31 = (bf16[2,64,1024]{2,1,0:T(8,128)(2,1)S(1)}, bf16[2,64,1024]{2,1,0:T(8,128)(2,1)S(1)}, u32[]{:S(2)}, u32[]{:S(2)}) collective-permute-start(bf16[2,64,1024]{2,1,0:T(8,128)(2,1)S(1)} %pad_maximum_fusion.8.refs_1_), channel_id=1, source_target_pairs={{0,4},{4,0},{8,12},{12,8},{16,20},{20,16},{24,28},{28,24},{1,5},{5... | collective-permute-start | bytes 786440 | tf_op jit(solution)/shard_map/A0c3m1/ppermute | solution.py:25
  71.1 4.6 %collective-permute-start.33 = (bf16[128,256]{1,0:T(8,128)(2,1)S(1)}, bf16[128,256]{1,0:T(8,128)(2,1)S(1)}, u32[]{:S(2)}, u32[]{:S(2)}) collective-permute-start(bf16[128,256]{1,0:T(8,128)(2,1)S(1)} %get-tuple-element.11), channel_id=1, source_target_pairs={{0,2},{1,3},{2,0},{3,1},{4,6},{5,7},{6,4},{7,5},{8,10},{9,11},{10,... | collective-permute-start | bytes 196616 | tf_op jit(solution)/shard_map/U0m2/ppermute | solution.py:25
  72.2 4.3 %collective-permute-start.34 = (bf16[128,256]{1,0:T(8,128)(2,1)S(1)}, bf16[128,256]{1,0:T(8,128)(2,1)S(1)}, u32[]{:S(2)}, u32[]{:S(2)}) collective-permute-start(bf16[128,256]{1,0:T(8,128)(2,1)S(1)} %get-tuple-element.12), channel_id=1, source_target_pairs={{0,3},{1,2},{2,1},{3,0},{4,7},{5,6},{6,5},{7,4},{8,11},{9,10},{10,... | collective-permute-start | bytes 196616 | tf_op jit(solution)/shard_map/U0m3/ppermute | solution.py:25
  72.2 4.3 %collective-permute-start.32 = (bf16[128,256]{1,0:T(8,128)(2,1)S(1)}, bf16[128,256]{1,0:T(8,128)(2,1)S(1)}, u32[]{:S(2)}, u32[]{:S(2)}) collective-permute-start(bf16[128,256]{1,0:T(8,128)(2,1)S(1)} %get-tuple-element.10), channel_id=1, source_target_pairs={{0,1},{1,0},{2,3},{3,2},{4,5},{5,4},{6,7},{7,6},{8,9},{9,8},{10,11... | collective-permute-start | bytes 196616 | tf_op jit(solution)/shard_map/U0m1/ppermute | solution.py:25
  (7 other events, 19.6 us)
